TPU v7x, 512 devices: a whole 4x4x16 slice. The times are simulated.
512 devices in a mesh: red: 64 (over z, y), rep: 8 (over x, core).
Axes of the slice: x: 4, y: 4, z: 16, core: 2. Of those that a mesh axis runs over, the one named last changes fastest.
Arguments:
- amplitudes: bfloat16 [7680, 960, 120], P(('rep', 'red')), may hold values from -6 to 6
- integrals: bfloat16 [960, 120, 8, 120], P('red', None, 'rep'), may hold values from -0.046875 to 0.046875
- other_terms: float32 [7680, 8, 120], P(('rep', 'red')), may hold values from -6 to 6
- occ_energy: float32 [120], replicated, may hold values from -2 to -0.5
- vir_energy: float32 [960], replicated, may hold values from 0.5 to 3
- occ_irrep: int32 [120], replicated, may hold values from 0 to 7, as said below
- vir_irrep: int32 [960], replicated, may hold values from 0 to 7, as said below
- slab_a: int32 [1], replicated, may hold values from 0 to 14
- slab_b: int32 [1], replicated, may hold values from 0 to 119
Outputs:
- new_amplitudes: float32 [7680, 8, 120], P(('rep', 'red'))
Inputs may be any that keep to these rules, and one draw needn't show every extreme that they name: `occ_irrep`: labels are nondecreasing over the orbitals (orbitals ordered by irrep); the first is 0 and the last is 7. `vir_irrep`: labels are nondecreasing over the orbitals (orbitals ordered by irrep); the first is 0 and the last is 7.
All inputs are finite; a program needn't handle non-finite values.
Results may differ from a plain program's by a relative error of at most 0.0003.
Values may be sent and summed in bfloat16 or wider, within the bound.
No kernel may reach another device: no remote copies, remote signals or barrier semaphores. Data moves between devices by JAX's collectives and lax.ppermute only.
A program may use at most 64 MiB of HBM per device.

v0:
```python
import jax
import jax.numpy as jnp
from jax import lax
from jax.sharding import PartitionSpec as P

A = 64
B = 8


def pair_labels(left, right):
    return jnp.bitwise_xor(left[:, None], right[None, :])


def on_device(
    amplitudes, integrals, other_terms, occ_energy, vir_energy, occ_irrep, vir_irrep, slab_a, slab_b
):
    red_count = lax.axis_size("red")
    rows_dev = amplitudes.shape[0]
    vir_local = integrals.shape[0]
    b_local = integrals.shape[2]
    occupied = occ_energy.shape[0]
    a_start = slab_a[0] * A
    b_start = slab_b[0] * B
    b_labels = lax.dynamic_slice_in_dim(vir_irrep, b_start, B)
    b_energy = lax.dynamic_slice_in_dim(vir_energy, b_start, B)
    c_labels = lax.dynamic_slice_in_dim(vir_irrep, lax.axis_index("red") * vir_local, vir_local)
    pair_ck = pair_labels(c_labels, occ_irrep)
    pair_bj = pair_labels(b_labels, occ_irrep)
    own_pairs = lax.dynamic_slice_in_dim(pair_bj, lax.axis_index("rep") * b_local, b_local, 0)
    local_kept = (pair_ck[:, :, None, None] == own_pairs[None, None]).astype(jnp.bfloat16)
    gathered = lax.all_gather(integrals * local_kept, "rep", axis=2, tiled=True)
    exchanged = lax.all_to_all(amplitudes, "red", split_axis=1, concat_axis=0, tiled=True)
    flat_amps = exchanged.reshape(exchanged.shape[0], vir_local * occupied)
    flat_ints = gathered.reshape(vir_local * occupied, B * occupied)
    mine = lax.psum_scatter(
        jnp.dot(flat_amps, flat_ints, preferred_element_type=jnp.float32),
        "red",
        scatter_dimension=0,
        tiled=True,
    )
    cycle_term = mine.reshape(rows_dev, B, occupied)
    first_global = (lax.axis_index("rep") * red_count + lax.axis_index("red")) * rows_dev
    row_ids = first_global + jnp.arange(rows_dev, dtype=jnp.int32)
    a_index = a_start + row_ids // occupied
    i_index = row_ids % occupied
    pair_ai = jnp.bitwise_xor(vir_irrep[a_index], occ_irrep[i_index])
    allowed = pair_ai[:, None, None] == pair_bj[None]
    row_energy = occ_energy[i_index] - vir_energy[a_index]
    col_energy = occ_energy[None, :] - b_energy[:, None]
    denominator = row_energy[:, None, None] + col_energy[None]
    updated = (cycle_term + other_terms) / denominator
    return jnp.where(allowed, updated, jnp.zeros_like(updated))


def solution(mesh):
    placed = (
        P(("rep", "red"), None, None),
        P("red", None, "rep", None),
        P(("rep", "red"), None, None),
        P(),
        P(),
        P(),
        P(),
        P(),
        P(),
    )
    return jax.shard_map(
        on_device,
        mesh=mesh,
        in_specs=placed,
        out_specs=P(("rep", "red"), None, None),
        check_vma=False,
    )
```

profile of v0, /device:TPU:6, one launch (start us, length us, event | category | flops | bytes accessed | tf_op | source)
XLA Modules:
  0.0 522.2 jit_solution(14917707788995452151)
XLA Ops:
  6.5 6.3 %copy.15 = bf16[15,960,120]{2,0,1:T(8,128)(2,1)} copy(bf16[15,960,120]{2,1,0:T(8,128)(2,1)} %param.9) | data formatting | bytes 6912000 | tf_op args[0]
  12.9 0.0 copy-start.2
  12.9 0.0 copy-start
  12.9 0.0 copy-start.4
  12.9 19.1 %all-to-all-start = ((bf16[15,960,120]{2,0,1:T(8,128)(2,1)}), bf16[15,960,120]{2,0,1:T(8,128)(2,1)}, u32[]{:S(2)}, u32[]{:S(2)}) async-start(bf16[15,960,120]{2,0,1:T(8,128)(2,1)} %copy.15), calls=%async_computation | async-start | bytes 7864320 | tf_op jit(solution)/shard_map/all_to_all | solution.py:32
  32.0 0.0 all-gather.2.cloned.1.call-start
  32.7 0.0 copy-done.2
  32.7 0.1 dynamic_slice.12
  32.8 0.1 dynamic_slice.13
  32.8 0.0 copy-done
  32.8 0.1 broadcast_xor_fusion.1
  32.9 0.1 broadcast_xor_fusion
  33.0 0.0 copy-done.4
  33.0 1.1 compare_select_fusion
  34.1 0.0 all-gather.2.cloned.1.call-update
  34.1 0.0 all-reduce.3.cloned.1.call-start
  34.2 37.5 %all-gather.2.cloned.1.call-done = bf16[15,120,8,120]{3,1,2,0:T(8,128)(2,1)} async-done(((bf16[15,120,1,120]{3,1,2,0:T(8,128)(2,1)}), bf16[15,120,8,120]{3,1,2,0:T(8,128)(2,1)}) %all-gather.2.cloned.1.call-update) | async-done | bytes 3456016 | tf_op jit(solution)/shard_map/all_gather | solution.py:31
  71.6 4.6 copy.14
  76.2 7.4 %reshape.177 = bf16[1800,960]{1,0:T(8,128)(2,1)} reshape(bf16[15,120,8,120]{3,2,1,0:T(8,128)(2,1)} %copy.14) | data formatting | bytes 6912000 | tf_op jit(solution)/shard_map/reshape | solution.py:34
  83.6 127.1 %all-to-all-done = bf16[15,960,120]{2,0,1:T(8,128)(2,1)} async-done(((bf16[15,960,120]{2,0,1:T(8,128)(2,1)}), bf16[15,960,120]{2,0,1:T(8,128)(2,1)}, u32[]{:S(2)}, u32[]{:S(2)}) %all-to-all-start) | async-done | bytes 3456032 | tf_op jit(solution)/shard_map/all_to_all | solution.py:32
  210.7 5.1 copy.17
  215.8 8.0 %reshape.178 = bf16[960,1800]{1,0:T(8,128)(2,1)} reshape(bf16[64,15,15,120]{3,2,1,0:T(8,128)(2,1)} %copy.17) | data formatting | bytes 6912000 | tf_op jit(solution)/shard_map/reshape | solution.py:33
  223.8 9.6 %convolution_bitcast_fusion = f32[960,960]{0,1:T(8,128)} fusion(bf16[1800,960]{1,0:T(8,128)(2,1)} %reshape.177, bf16[960,1800]{1,0:T(8,128)(2,1)} %reshape.178), kind=kOutput, calls=%fused_computation.4 | convolution fusion | flops 3317760000 | bytes 10598400 | tf_op jit(solution)/shard_map/dot_general | solution.py:36
  233.4 0.0 copy-start.3
  233.4 0.0 copy-start.1
  233.4 0.0 copy-start.5
  233.4 0.0 all-reduce.3.cloned.1.call-update
  234.2 0.6 gather_fusion
  234.8 0.0 copy-done.3
  234.8 0.6 gather_fusion.3
  235.5 0.1 dynamic_slice.15
  235.5 0.7 gather_fusion.1
  236.2 0.0 copy-done.1
  236.2 0.7 gather_fusion.2
  236.9 1.3 dynamic-slice
  238.8 0.1 broadcast_subtract_fusion
  238.9 274.1 %all-reduce.3.cloned.1.call-done = f32[960,960]{0,1:T(8,128)} async-done(((f32[960,960]{0,1:T(8,128)}), f32[960,960]{0,1:T(8,128)}) %all-reduce.3.cloned.1.call-update) | async-done | bytes 3686416
  513.0 1.4 constant_dynamic-slice_fusion
  514.4 0.2 copy.18
  514.6 0.0 copy-done.5
  514.6 0.7 divide_select_fusion
  (6 shorter events, 0.0 us)
Async XLA Ops:
  12.9 19.8 %copy-start.2 = (s32[960]{0:T(1024)S(1)}, s32[960]{0:T(1024)}, u32[]{:S(2)}) copy-start(s32[960]{0:T(1024)} %param.15) | copy-start | bytes 11524
  12.9 20.0 %copy-start = (s32[120]{0:T(128)S(1)}, s32[120]{0:T(128)}, u32[]{:S(2)}) copy-start(s32[120]{0:T(128)} %param.14) | copy-start | bytes 1444
  12.9 20.1 %copy-start.4 = (bf16[15,120,1,120]{3,1,2,0:T(8,128)(2,1)S(1)}, bf16[15,120,1,120]{3,1,2,0:T(8,128)(2,1)}, u32[]{:S(2)}) copy-start(bf16[15,120,1,120]{3,1,2,0:T(8,128)(2,1)} %param.10) | copy-start | bytes 1296004
  12.9 197.9 %all-to-all-start = ((bf16[15,960,120]{2,0,1:T(8,128)(2,1)}), bf16[15,960,120]{2,0,1:T(8,128)(2,1)}, u32[]{:S(2)}, u32[]{:S(2)}) async-start(bf16[15,960,120]{2,0,1:T(8,128)(2,1)} %copy.15), calls=%async_computation | async-start | bytes 7864320 | tf_op jit(solution)/shard_map/all_to_all | solution.py:32
  32.0 39.7 %all-gather.2.cloned.1.call-start = ((), (), s32[]{:S(2)}) async-start(), calls=%async_computation.1 | async-start | bytes 4147200 | tf_op jit(solution)/shard_map/all_gather | solution.py:31
  34.1 478.9 %all-reduce.3.cloned.1.call-start = ((), (), s32[]{:S(2)}) async-start(), calls=%async_computation.2 | async-start | bytes 7864320
  233.4 1.4 copy-start.3
  233.4 2.8 copy-start.1
  233.4 281.2 %copy-start.5 = (f32[15,8,120]{2,1,0:T(8,128)S(1)}, f32[15,8,120]{2,1,0:T(8,128)}, u32[]{:S(2)}) copy-start(f32[15,8,120]{2,1,0:T(8,128)} %param.11) | copy-start | bytes 172804
Sparse Core Ops, SparseCore 0:
  34.9 36.6 all-gather.1
  233.6 279.4 all-reduce.2
where the time goes:
time: 523 us; the launch traced here: 522 us
  waiting for transfers between devices  439 us (84%)
  local copies, waits for them, and re-layouts  37.1 us (7%)
  starting transfers between devices  19.2 us (4%)
  between operations  15.5 us (3%)
  matrix products  9.59 us (2%)
    unnamed x3, waiting for transfers between devices  274 us
    all_to_all x1, waiting for transfers between devices, on_device(): lax.all_to_all(amplitudes, 'red', split_axis=1, concat_axis=0, tiled=True)  127 us
    all_gather x1, waiting for transfers between devices, on_device(): gathered = lax.all_gather(integrals * local_kept, 'rep', axis=2, tiled=True)  37.5 us
    all_to_all x1, starting transfers between devices, on_device(): lax.all_to_all(amplitudes, 'red', split_axis=1, concat_axis=0, tiled=True)  19.1 us
  transfers between devices with their start and end apart: 3, of which 3 were waited for; matrix products, arithmetic and copies ran while one was open for 3% of the time, Pallas kernels for 0%

commit v1 on v0

v1 whole, which is shorter than its diff:
```python
import functools

import jax
import jax.numpy as jnp
from jax import lax
from jax.experimental import pallas as pl
from jax.experimental.pallas import tpu as pltpu
from jax.sharding import Mesh, PartitionSpec as P

A = 64
B = 8
O = 120
V = 960
ROWS = 15
SLOTS = 24
GROUP = 5
PARTS = ROWS // GROUP
FAR = 4
NEAR = 16
REP = 8
LANES = 128
BF = jnp.bfloat16
F32 = jnp.float32


def pair_labels(left, right):
    return jnp.bitwise_xor(left[:, None], right[None, :])


def column_of(row):
    n = row.shape[1]
    same = lax.broadcasted_iota(jnp.int32, (n, n), 0) == lax.broadcasted_iota(jnp.int32, (n, n), 1)
    return jnp.sum(jnp.where(same, row.astype(F32), 0.0), axis=1, keepdims=True).astype(jnp.int32)


def positions(occ_row):
    n = occ_row.shape[1]
    occ_col = column_of(occ_row)
    k_col = lax.broadcasted_iota(jnp.int32, (n, n), 0)
    k_row = lax.broadcasted_iota(jnp.int32, (n, n), 1)
    same = occ_col == occ_row
    row = jnp.sum(jnp.where(same & (k_col < k_row), 1.0, 0.0), axis=0, keepdims=True)
    col = jnp.sum(jnp.where(same & (k_row < k_col), 1.0, 0.0), axis=1, keepdims=True)
    return occ_col, row.astype(jnp.int32), col.astype(jnp.int32)


def thirds(x):
    high = x.astype(BF)
    rest = x - high.astype(F32)
    middle = rest.astype(BF)
    low = (rest - middle.astype(F32)).astype(BF)
    return high, middle, low


def pack_integrals(place, vir_irrep, slab_b, occ_row, integrals, out, scratch):
    red, rep = place()
    occ = occ_row[...]
    occ_col, pos_row, _ = positions(occ)
    slot = lax.broadcasted_iota(jnp.int32, (SLOTS, O), 0)
    pick = jnp.where(slot == pos_row, 1.0, 0.0).astype(BF)
    b_label = vir_irrep[slab_b[0] * B + rep]
    scratch[...] = jnp.zeros_like(scratch)
    for c in range(ROWS):
        label = vir_irrep[red * ROWS + c] ^ b_label
        kept = jnp.where((occ_col ^ label) == occ, integrals[c].astype(F32), 0.0).astype(BF)
        first = LANES * (c // GROUP) + SLOTS * (c % GROUP)
        scratch[first : first + SLOTS, :O] = jnp.dot(pick, kept, preferred_element_type=F32)
    out[...] = scratch[...].astype(BF)


def pack_amplitudes(
    place, vir_irrep, occ_irrep, slab_a, occ_row, vir_rows, amplitudes, out, starts, chosen, row, packed
):
    red, rep = place()
    step = pl.program_id(0)
    occ = occ_row[...]

    @pl.when(step == 0)
    def _():
        _, _, pos_col = positions(occ)
        lane = lax.broadcasted_iota(jnp.int32, (O, LANES), 1)
        for u in range(GROUP):
            hit = (lane == pos_col + SLOTS * u) & (pos_col < SLOTS)
            chosen[u, :O] = jnp.where(hit, 1.0, 0.0).astype(BF)
        labels = vir_rows[...]
        for g in range(9):
            below = jnp.sum(jnp.where(labels < g, 1.0, 0.0), axis=1, keepdims=True)
            starts[g : g + 1] = jnp.broadcast_to(
                jnp.sum(below, axis=0, keepdims=True).astype(jnp.int32), (1, LANES)
            )
        packed[pl.ds(ROWS, V // GROUP, stride=16), :] = jnp.zeros((V // GROUP, LANES), F32)

    row_id = (rep * (FAR * NEAR) + red) * ROWS + step
    label = vir_irrep[slab_a[0] * A + row_id // O] ^ occ_irrep[row_id % O]
    partner = occ ^ label
    low = jnp.zeros((1, O), jnp.int32)
    high = jnp.zeros((1, O), jnp.int32)
    for g in range(8):
        low = jnp.where(partner == g, starts[g : g + 1, :O], low)
        high = jnp.where(partner == g, starts[g + 1 : g + 2, :O], high)
    c_index = lax.broadcasted_iota(jnp.int32, (V, O), 0)
    kept = (c_index >= low) & (c_index < high)
    row[:, :O] = jnp.where(kept, amplitudes[0].astype(F32), 0.0)
    total = jnp.zeros((V // GROUP, LANES), F32)
    for u in range(GROUP):
        part = row[pl.ds(u, V // GROUP, stride=GROUP), :]
        total += jnp.dot(part[:, :O].astype(BF), chosen[u, :O], preferred_element_type=F32)
    packed[pl.ds(step, V // GROUP, stride=16), :] = total

    @pl.when(step == ROWS - 1)
    def _():
        rows = PARTS * 16
        for e in range(NEAR):
            for far in range(FAR):
                first = (far * NEAR + e) * rows
                out[e, far * rows : (far + 1) * rows] = packed[first : first + rows].astype(BF)


def multiply(place, vir_irrep, slab_a, slab_b, occ_row, vir_rows, amps, ints, out, left):
    red, rep = place()
    far_own = red // NEAR
    occ = occ_row[...]
    _, _, pos_col = positions(occ)
    rows = NEAR * 16
    for s in range(NEAR):
        for block in range(FAR * PARTS):
            left[s * 16 : (s + 1) * 16, block * LANES : (block + 1) * LANES] = amps[
                s, block * 16 : (block + 1) * 16
            ]
    row = lax.broadcasted_iota(jnp.int32, (rows, 1), 0)
    local = (row // 16) * ROWS + row % 16
    second = local >= O
    i_index = jnp.where(second, local - O, local)
    i_label = jnp.zeros((rows, 1), jnp.int32)
    for g in range(1, 8):
        start = jnp.sum(jnp.where(occ < g, 1.0, 0.0), axis=1, keepdims=True).astype(jnp.int32)
        i_label += jnp.where(i_index >= start, 1, 0)
    a_first = slab_a[0] * A + (rep * FAR + far_own) * 2
    row_label = i_label ^ jnp.where(second, vir_irrep[a_first + 1], vir_irrep[a_first])
    lane = lax.broadcasted_iota(jnp.int32, (O, LANES), 1)
    main = jnp.zeros((rows, LANES), F32)
    rest = jnp.zeros((rows, LANES), F32)
    amounts = left[...]
    for pair in range(B // 2):
        right = jnp.concatenate([ints[2 * pair], ints[2 * pair + 1]], axis=1)
        both = jnp.dot(amounts, right, preferred_element_type=F32)
        for half in range(2):
            b = 2 * pair + half
            b_label = vir_irrep[slab_b[0] * B + b]
            part = both[:, half * LANES : half * LANES + O]
            part = jnp.where((row_label ^ b_label) == occ, part, 0.0)
            pieces = thirds(part)
            if SLOTS * b < LANES:
                pick = jnp.where(lane == pos_col + SLOTS * b, 1.0, 0.0).astype(BF)
                for piece in pieces:
                    main += jnp.dot(piece, pick, preferred_element_type=F32)
            if SLOTS * (b + 1) > LANES:
                pick = jnp.where(lane == pos_col + (SLOTS * b - LANES), 1.0, 0.0).astype(BF)
                for piece in pieces:
                    rest += jnp.dot(piece, pick, preferred_element_type=F32)
    moved = pltpu.roll(rest, LANES // 2, 1)
    for e in range(NEAR):
        out[e, :16] = main[e * 16 : (e + 1) * 16]
        out[e, 16:] = rest[e * 16 : e * 16 + 8] + moved[e * 16 + 8 : e * 16 + 16]


def finish(
    place, vir_irrep, occ_irrep, slab_a, slab_b, occ_energy, vir_energy, occ_row, energy_row, parts, other, out, cycle
):
    red, rep = place()
    occ = occ_row[...]
    _, pos_row, _ = positions(occ)
    total = parts[0]
    for s in range(1, NEAR):
        total += parts[s]
    main = total[:16]
    rest = jnp.concatenate([total[16:], pltpu.roll(total[16:], LANES // 2, 1)], axis=0)
    mains = jnp.concatenate(thirds(main), axis=0)
    rests = jnp.concatenate(thirds(rest), axis=0)
    lane = lax.broadcasted_iota(jnp.int32, (LANES, O), 0)
    for b in range(B):
        value = jnp.zeros((48, O), F32)
        if SLOTS * b < LANES:
            pick = jnp.where(lane == pos_row + SLOTS * b, 1.0, 0.0).astype(BF)
            value += jnp.dot(mains, pick, preferred_element_type=F32)
        if SLOTS * (b + 1) > LANES:
            at = pos_row + (SLOTS * b - LANES)
            pick = jnp.where((lane == at) & (lane < LANES // 2), 1.0, 0.0).astype(BF)
            value += jnp.dot(rests, pick, preferred_element_type=F32)
        cycle[pl.ds(b, 16, stride=B), :O] = (value[:16] + value[16:32]) + value[32:]
    b_first = slab_b[0] * B
    b_index = lax.broadcasted_iota(jnp.int32, (B, 1), 0)
    b_label = jnp.zeros((B, 1), jnp.int32)
    b_energy = jnp.zeros((B, 1), F32)
    for b in range(B):
        b_label = jnp.where(b_index == b, vir_irrep[b_first + b], b_label)
        b_energy = jnp.where(b_index == b, vir_energy[b_first + b], b_energy)
    pair_bj = b_label ^ occ
    col_energy = energy_row[...] - b_energy
    for r in range(ROWS):
        row_id = (rep * (FAR * NEAR) + red) * ROWS + r
        a = slab_a[0] * A + row_id // O
        i = row_id % O
        label = vir_irrep[a] ^ occ_irrep[i]
        row_energy = occ_energy[i] - vir_energy[a]
        updated = (cycle[r * B : (r + 1) * B, :O] + other[r]) / (row_energy + col_energy)
        out[r] = jnp.where(pair_bj == label, updated, 0.0)


def own_place():
    return lax.axis_index("far") * NEAR + lax.axis_index("near"), lax.axis_index("rep")


SMEM = pl.BlockSpec(memory_space=pltpu.SMEM)
VMEM = pl.BlockSpec(memory_space=pltpu.VMEM)


def params(limit):
    return pltpu.CompilerParams(vmem_limit_bytes=limit * 1024 * 1024)


def call_pack_integrals(place, vir_irrep, slab_b, occ_row, integrals, **kw):
    return pl.pallas_call(
        functools.partial(pack_integrals, place),
        out_shape=jax.ShapeDtypeStruct((PARTS * LANES, LANES), BF),
        in_specs=[SMEM, SMEM, VMEM, VMEM],
        out_specs=VMEM,
        scratch_shapes=[pltpu.VMEM((PARTS * LANES, LANES), F32)],
        compiler_params=params(16),
        cost_estimate=pl.CostEstimate(flops=2 * 10**7, bytes_accessed=600000, transcendentals=0),
        name="pack_integrals",
        **kw,
    )(vir_irrep, slab_b, occ_row, integrals)


def call_pack_amplitudes(place, vir_irrep, occ_irrep, slab_a, occ_row, vir_rows, amplitudes, **kw):
    fixed = lambda shape: pl.BlockSpec(shape, lambda r: (0,) * len(shape))
    return pl.pallas_call(
        functools.partial(pack_amplitudes, place),
        out_shape=jax.ShapeDtypeStruct((NEAR, FAR * PARTS * 16, LANES), BF),
        grid=(ROWS,),
        in_specs=[SMEM, SMEM, SMEM, fixed((1, O)), fixed((B, O)), pl.BlockSpec((1, V, O), lambda r: (r, 0, 0))],
        out_specs=fixed((NEAR, FAR * PARTS * 16, LANES)),
        scratch_shapes=[
            pltpu.VMEM((16, LANES), jnp.int32),
            pltpu.VMEM((GROUP, LANES, LANES), BF),
            pltpu.VMEM((V, LANES), F32),
            pltpu.VMEM((V // GROUP * 16, LANES), F32),
        ],
        compiler_params=params(32),
        cost_estimate=pl.CostEstimate(flops=10**9, bytes_accessed=4500000, transcendentals=0),
        name="pack_amplitudes",
        **kw,
    )(vir_irrep, occ_irrep, slab_a, occ_row, vir_rows, amplitudes)


def call_multiply(place, vir_irrep, slab_a, slab_b, occ_row, vir_rows, amps, ints, **kw):
    return pl.pallas_call(
        functools.partial(multiply, place),
        out_shape=jax.ShapeDtypeStruct((NEAR, 24, LANES), F32),
        in_specs=[SMEM, SMEM, SMEM, VMEM, VMEM, VMEM, VMEM],
        out_specs=VMEM,
        scratch_shapes=[pltpu.VMEM((NEAR * 16, FAR * PARTS * LANES), BF)],
        compiler_params=params(48),
        name="multiply",
        **kw,
    )(vir_irrep, slab_a, slab_b, occ_row, vir_rows, amps, ints)


def call_finish(place, vir_irrep, occ_irrep, slab_a, slab_b, occ_energy, vir_energy, occ_row, energy_row, parts, other, **kw):
    return pl.pallas_call(
        functools.partial(finish, place),
        out_shape=jax.ShapeDtypeStruct((ROWS, B, O), F32),
        in_specs=[SMEM] * 6 + [VMEM] * 4,
        out_specs=VMEM,
        scratch_shapes=[pltpu.VMEM((16 * B, LANES), F32)],
        compiler_params=params(16),
        name="finish",
        **kw,
    )(vir_irrep, occ_irrep, slab_a, slab_b, occ_energy, vir_energy, occ_row, energy_row, parts, other)


def packed_form(amplitudes, integrals, other_terms, occ_energy, vir_energy, occ_irrep, vir_irrep, slab_a, slab_b):
    occ_row = occ_irrep.reshape(1, O)
    vir_rows = vir_irrep.reshape(B, O)
    ints = call_pack_integrals(own_place, vir_irrep, slab_b, occ_row, integrals.reshape(ROWS, O, O))
    ints = lax.all_gather(ints, "far", axis=0, tiled=True)
    ints = lax.all_gather(ints, "rep", axis=0)
    amps = call_pack_amplitudes(own_place, vir_irrep, occ_irrep, slab_a, occ_row, vir_rows, amplitudes)
    amps = lax.all_to_all(amps, "near", 0, 0, tiled=True)
    parts = call_multiply(own_place, vir_irrep, slab_a, slab_b, occ_row, vir_rows, amps, ints)
    parts = lax.all_to_all(parts, "near", 0, 0, tiled=True)
    return call_finish(
        own_place, vir_irrep, occ_irrep, slab_a, slab_b, occ_energy, vir_energy,
        occ_row, occ_energy.reshape(1, O), parts, other_terms,
    )


def whole_form(amplitudes, integrals, other_terms, occ_energy, vir_energy, occ_irrep, vir_irrep, slab_a, slab_b):
    red = ("far", "near")
    red_count = FAR * NEAR
    rows_dev = amplitudes.shape[0]
    vir_local = integrals.shape[0]
    b_local = integrals.shape[2]
    occupied = occ_energy.shape[0]
    a_start = slab_a[0] * A
    b_start = slab_b[0] * B
    b_labels = lax.dynamic_slice_in_dim(vir_irrep, b_start, B)
    b_energy = lax.dynamic_slice_in_dim(vir_energy, b_start, B)
    c_labels = lax.dynamic_slice_in_dim(vir_irrep, lax.axis_index(red) * vir_local, vir_local)
    pair_ck = pair_labels(c_labels, occ_irrep)
    pair_bj = pair_labels(b_labels, occ_irrep)
    own_pairs = lax.dynamic_slice_in_dim(pair_bj, lax.axis_index("rep") * b_local, b_local, 0)
    local_kept = (pair_ck[:, :, None, None] == own_pairs[None, None]).astype(jnp.bfloat16)
    gathered = lax.all_gather(integrals * local_kept, "rep", axis=2, tiled=True)
    exchanged = lax.all_to_all(amplitudes, red, split_axis=1, concat_axis=0, tiled=True)
    flat_amps = exchanged.reshape(exchanged.shape[0], vir_local * occupied)
    flat_ints = gathered.reshape(vir_local * occupied, B * occupied)
    mine = lax.psum_scatter(
        jnp.dot(flat_amps, flat_ints, preferred_element_type=jnp.float32),
        red,
        scatter_dimension=0,
        tiled=True,
    )
    cycle_term = mine.reshape(rows_dev, B, occupied)
    first_global = (lax.axis_index("rep") * red_count + lax.axis_index(red)) * rows_dev
    row_ids = first_global + jnp.arange(rows_dev, dtype=jnp.int32)
    a_index = a_start + row_ids // occupied
    i_index = row_ids % occupied
    pair_ai = jnp.bitwise_xor(vir_irrep[a_index], occ_irrep[i_index])
    allowed = pair_ai[:, None, None] == pair_bj[None]
    row_energy = occ_energy[i_index] - vir_energy[a_index]
    col_energy = occ_energy[None, :] - b_energy[:, None]
    denominator = row_energy[:, None, None] + col_energy[None]
    updated = (cycle_term + other_terms) / denominator
    return jnp.where(allowed, updated, jnp.zeros_like(updated))


def on_device(*args):
    occ_irrep = args[5]
    crowded = jnp.any(occ_irrep[SLOTS:] == occ_irrep[:-SLOTS])
    return lax.cond(crowded, whole_form, packed_form, *args)


def solution(mesh):
    split = Mesh(mesh.devices.reshape(FAR, NEAR, REP), ("far", "near", "rep"))
    placed = (
        P(("rep", "far", "near"), None, None),
        P(("far", "near"), None, "rep", None),
        P(("rep", "far", "near"), None, None),
        P(),
        P(),
        P(),
        P(),
        P(),
        P(),
    )
    return jax.shard_map(
        on_device,
        mesh=split,
        in_specs=placed,
        out_specs=P(("rep", "far", "near"), None, None),
        check_vma=False,
    )
```

time: 523 us -> 109 us (0.21)
  waiting for transfers between devices: 439 us -> 0.02 us
  blocking collectives: 0 us -> 68.4 us
  local copies, waits for them, and re-layouts: 37.1 us -> 3.3 us
  Pallas kernels: 0 us -> 20.7 us
  starting transfers between devices: 19.2 us -> 0.04 us
  matrix products: 9.59 us -> 0 us
    unnamed x3 -> x0, waiting for transfers between devices: 274 us -> none
    all_to_all x1 -> x0, waiting for transfers between devices: 127 us -> none  [on_device(): lax.all_to_all(amplitudes, 'red', split_axis=1, concat_axis=0, tiled=True)]
    all_to_all x0 -> x2, blocking collectives: none -> 37.7 us  [the longest x1 24.3 us: packed_form(): amps = lax.all_to_all(amps, 'near', 0, 0, tiled=True)]
    all_gather x1, waiting for transfers between devices: 37.5 us -> 0.01 us  [packed_form(): ints = lax.all_gather(ints, 'rep', axis=0)]
    all_gather x0 -> x1, blocking collectives: none -> 30.7 us  [packed_form(): ints = lax.all_gather(ints, 'far', axis=0, tiled=True)]
    pallas_call x0 -> x4, Pallas kernels: none -> 20.7 us  [the longest x1 12 us: call_pack_amplitudes(): pl.pallas_call(functools.partial(pack_amplitudes, place), out_shape=jax.S...]
    all_to_all x1 -> x0, starting transfers between devices: 19.1 us -> none  [on_device(): lax.all_to_all(amplitudes, 'red', split_axis=1, concat_axis=0, tiled=True)]
    reshape x3 -> x1, local copies, waits for them, and re-layouts: 15.6 us -> 0.76 us  [packed_form(): vir_rows = vir_irrep.reshape(B, O)]
  transfers between devices with their start and end apart: 3 -> 1, of which waited for: 3 -> 0; matrix products, arithmetic and copies ran while one was open for 3% -> 1% of each run, Pallas kernels for 0% -> 11%
where the time goes in v1:
time: 109 us; the launch traced here: 108 us
  blocking collectives  68.4 us (63%)
  Pallas kernels  20.7 us (19%)
  between operations  14 us (13%)
  local copies, waits for them, and re-layouts  3.3 us (3%)
  other arithmetic  1.44 us (1%)
    all_gather x1, blocking collectives, packed_form(): ints = lax.all_gather(ints, 'far', axis=0, tiled=True)  30.7 us
    all_to_all x1, blocking collectives, packed_form(): amps = lax.all_to_all(amps, 'near', 0, 0, tiled=True)  24.3 us
    all_to_all x1, blocking collectives, packed_form(): parts = lax.all_to_all(parts, 'near', 0, 0, tiled=True)  13.4 us
    pallas_call x1, Pallas kernels, call_pack_amplitudes(): pl.pallas_call(functools.partial(pack_amplitudes, place), out_shape=jax.S...  12 us
    pallas_call x1, Pallas kernels, call_multiply(): pl.pallas_call(functools.partial(multiply, place), out_shape=jax.ShapeDty...  4.38 us
    pallas_call x1, Pallas kernels, call_finish(): pl.pallas_call(functools.partial(finish, place), out_shape=jax.ShapeDtype...  2.34 us
  transfers between devices with their start and end apart: 1, of which 0 were waited for; matrix products, arithmetic and copies ran while one was open for 1% of the time, Pallas kernels for 11%

profile of v1, /device:TPU:6, one launch (start us, length us, event | category | flops | bytes accessed | tf_op | source)
XLA Modules:
  0.0 108.3 jit_solution(6892929887221479128)
XLA Ops:
  6.5 1.4 %compare_reduce_fusion = pred[]{:T(512)} fusion(s32[120]{0:T(128)} %param.16), kind=kLoop, calls=%fused_computation.22 | loop fusion | flops 191 | bytes 769 | tf_op jit(solution)/shard_map/reduce_or | solution.py:341
  8.6 92.2 %conditional.1 = (f32[15,8,120]{2,1,0:T(8,128)S(1)}) conditional(s32[]{:T(128)} %convert_element_type.4, (s32[120]{0:T(128)}, f32[120]{0:T(128)}, s32[960]{0:T(1024)}, s32[1]{0:T(128)}, bf16[15,960,120]{2,1,0:T(8,128)(2,1)}, /*index=5*/bf16[15,120,1,120]{3,1,2,0:T(8,128)(2,1)}, s32[1]{0:T(128)}, f32[960]{0:T(1024)}, ...), branch_computations={%region_1.0_spmd, %region_2.4_spmd} | conditional | flops 3319191552 | bytes 94430496 | solution.py:342
  8.6 0.0 all-gather.4.cloned.1.call-start
  8.7 0.0 copy-start.1
  8.7 0.0 copy-start.5
  8.7 2.0 %pack_integrals.1 = bf16[384,128]{1,0:T(8,128)(2,1)S(1)} custom-call(s32[960]{0:T(1024)} %get-tuple-element.44.vir_irrep, s32[1]{0:T(128)} %get-tuple-element.47.slab_b, s32[1,120]{1,0:T(1,128)} %bitcast.30, bf16[15,120,120]{2,1,0:T(8,128)(2,1)} %bitcast.36), custom_call_target="tpu_custom_call" | custom-call | flops 20000000 | bytes 600000 | tf_op jit(solution)/shard_map/cond/branch_0_fun/pack_integrals/pallas_call | solution.py:223
  10.8 30.7 %all_gather.8 = bf16[1536,128]{1,0:T(8,128)(2,1)} all-gather(bf16[384,128]{1,0:T(8,128)(2,1)S(1)} %pack_integrals.1), channel_id=1, replica_groups=mesh['far'=4,'near'=16,'rep'=8] {'far'}, dimensions={0}, use_global_device_ids=true | all-gather | bytes 491520 | tf_op jit(solution)/shard_map/cond/branch_0_fun/all_gather | solution.py:287
  41.4 0.0 all-gather.4.cloned.1.call-update
  41.5 0.8 reshape.184.vir_rows
  42.2 12.0 %pack_amplitudes.1 = bf16[16,192,128]{2,1,0:T(8,128)(2,1)S(1)} custom-call(s32[960]{0:T(1024)} %get-tuple-element.44.vir_irrep, s32[120]{0:T(128)} %get-tuple-element.45.occ_irrep, s32[1]{0:T(128)} %get-tuple-element.46.slab_a, s32[1,120]{1,0:T(1,128)} %bitcast.31, s32[8,120]{1,0:T(8,128)S(1)} %reshape.184.vir_rows, ...), custom_call_target="tpu_custom_call" | custom-call | flops 1000000000 | bytes 4500000 | tf_op jit(solution)/shard_map/cond/branch_0_fun/pack_amplitudes/pallas_call | solution.py:238
  54.2 0.0 copy-start.3
  54.2 0.0 copy-start.7
  54.2 0.0 copy-start.10
  54.2 24.3 %all_to_all.20.amps = bf16[16,192,128]{2,1,0:T(8,128)(2,1)S(1)} all-to-all(bf16[16,192,128]{2,1,0:T(8,128)(2,1)S(1)} %pack_amplitudes.1), channel_id=1, replica_groups=mesh['far'=4,'near'=16,'rep'=8] {'near'}, dimensions={0} | all-to-all | bytes 1572864 | tf_op jit(solution)/shard_map/cond/branch_0_fun/all_to_all | solution.py:290
  78.5 0.0 all-gather.4.cloned.1.call-done
  78.5 0.0 copy-done.1
  78.5 0.0 copy-done.5
  78.5 0.0 copy-start
  78.6 1.9 %copy-done = bf16[12288,128]{1,0:T(8,128)(2,1)S(1)} copy-done((bf16[12288,128]{1,0:T(8,128)(2,1)S(1)}, bf16[12288,128]{1,0:T(8,128)(2,1)}, u32[]{:S(2)}) %copy-start) | copy-done | bytes 3145752 | tf_op jit(solution)/shard_map/cond
  80.4 4.4 %multiply.3 = f32[16,24,128]{2,1,0:T(8,128)S(1)} custom-call(s32[960]{0:T(1024)S(1)} %copy-done.5, s32[1]{0:T(128)} %get-tuple-element.46.slab_a, s32[1]{0:T(128)} %get-tuple-element.47.slab_b, s32[1,120]{1,0:T(1,128)S(1)} %bitcast.32, s32[8,120]{1,0:T(8,128)S(1)} %reshape.184.vir_rows, bf16[16,192,128]{2,1,0:T(8,128)(2,1)S(1)} %all_to_all.20.amps, ...), custom_call_target="tpu_custom_call" | custom-call | tf_op jit(solution)/shard_map/cond/branch_0_fun/multiply/pallas_call | solution.py:258
  84.8 13.4 %all_to_all.21.parts = f32[16,24,128]{2,1,0:T(8,128)S(1)} all-to-all(f32[16,24,128]{2,1,0:T(8,128)S(1)} %multiply.3), channel_id=1, replica_groups=mesh['far'=4,'near'=16,'rep'=8] {'near'}, dimensions={0} | all-to-all | bytes 393216 | tf_op jit(solution)/shard_map/cond/branch_0_fun/all_to_all | solution.py:292
  98.2 0.0 copy-done.3
  98.2 0.0 copy-done.7
  98.2 0.0 copy-done.10
  98.2 2.3 %finish.1 = f32[15,8,120]{2,1,0:T(8,128)S(1)} custom-call(s32[960]{0:T(1024)S(1)} %copy-done.5, s32[120]{0:T(128)S(1)} %copy-done.1, s32[1]{0:T(128)} %get-tuple-element.46.slab_a, s32[1]{0:T(128)} %get-tuple-element.47.slab_b, f32[120]{0:T(128)S(1)} %copy-done.3, f32[960]{0:T(1024)S(1)} %copy-done.7, s32[1,120]{1,0:T(1,128)S(1)} %bitcast.33, ...), custom_call_target="tpu_custom_call" | custom-call | tf_op jit(solution)/shard_map/cond/branch_0_fun/finish/pallas_call | solution.py:271
  100.8 0.0 copy-start.12
  100.8 0.6 copy-done.12
Async XLA Ops:
  8.6 69.9 %all-gather.4.cloned.1.call-start = ((), (), s32[]{:S(2)}) async-start(), calls=%async_computation.3 | async-start | bytes 3538944 | tf_op jit(solution)/shard_map/cond/branch_0_fun/all_gather | solution.py:288
  8.7 69.9 %copy-start.1 = (s32[120]{0:T(128)S(1)}, s32[120]{0:T(128)}, u32[]{:S(2)}) copy-start(s32[120]{0:T(128)} %get-tuple-element.45.occ_irrep) | copy-start | bytes 1444 | tf_op jit(solution)/shard_map/cond
  8.7 69.8 %copy-start.5 = (s32[960]{0:T(1024)S(1)}, s32[960]{0:T(1024)}, u32[]{:S(2)}) copy-start(s32[960]{0:T(1024)} %get-tuple-element.44.vir_irrep) | copy-start | bytes 11524 | tf_op jit(solution)/shard_map/cond
  54.2 44.0 %copy-start.3 = (f32[120]{0:T(128)S(1)}, f32[120]{0:T(128)}, u32[]{:S(2)}) copy-start(f32[120]{0:T(128)} %get-tuple-element.48.occ_energy) | copy-start | bytes 1444 | tf_op jit(solution)/shard_map/cond
  54.2 44.0 %copy-start.7 = (f32[960]{0:T(1024)S(1)}, f32[960]{0:T(1024)}, u32[]{:S(2)}) copy-start(f32[960]{0:T(1024)} %get-tuple-element.49.vir_energy) | copy-start | bytes 11524 | tf_op jit(solution)/shard_map/cond
  54.2 44.0 %copy-start.10 = (f32[15,8,120]{2,1,0:T(8,128)S(1)}, f32[15,8,120]{2,1,0:T(8,128)}, u32[]{:S(2)}) copy-start(f32[15,8,120]{2,1,0:T(8,128)} %get-tuple-element.52.other) | copy-start | bytes 172804 | tf_op jit(solution)/shard_map/cond
  78.5 1.9 %copy-start = (bf16[12288,128]{1,0:T(8,128)(2,1)S(1)}, bf16[12288,128]{1,0:T(8,128)(2,1)}, u32[]{:S(2)}) copy-start(bf16[12288,128]{1,0:T(8,128)(2,1)} %all-gather.4.cloned.1.call-done) | copy-start | bytes 9437188 | tf_op jit(solution)/shard_map/cond
  100.8 0.6 copy-start.12
Sparse Core Ops, SparseCore 0:
  41.6 30.4 all-gather.3

commit v2 on v1

--- a/solution.py
+++ b/solution.py
@@ -15,6 +15,7 @@
 SLOTS = 24
 GROUP = 5
 PARTS = ROWS // GROUP
+STEP = 5
 FAR = 4
 NEAR = 16
 REP = 8
@@ -69,7 +70,7 @@
 
 
 def pack_amplitudes(
-    place, vir_irrep, occ_irrep, slab_a, occ_row, vir_rows, amplitudes, out, starts, chosen, row, packed
+    place, vir_irrep, occ_irrep, slab_a, occ_row, vir_rows, amplitudes, out, most, starts, chosen, row, packed
 ):
     red, rep = place()
     step = pl.program_id(0)
@@ -77,11 +78,13 @@
 
     @pl.when(step == 0)
     def _():
-        _, _, pos_col = positions(occ)
+        _, pos_row, pos_col = positions(occ)
+        most[0, 0] = jnp.max(pos_row)
         lane = lax.broadcasted_iota(jnp.int32, (O, LANES), 1)
+        chosen[...] = jnp.zeros_like(chosen)
         for u in range(GROUP):
             hit = (lane == pos_col + SLOTS * u) & (pos_col < SLOTS)
-            chosen[u, :O] = jnp.where(hit, 1.0, 0.0).astype(BF)
+            chosen[u * LANES : u * LANES + O] = jnp.where(hit, 1.0, 0.0).astype(BF)
         labels = vir_rows[...]
         for g in range(9):
             below = jnp.sum(jnp.where(labels < g, 1.0, 0.0), axis=1, keepdims=True)
@@ -89,25 +92,28 @@
                 jnp.sum(below, axis=0, keepdims=True).astype(jnp.int32), (1, LANES)
             )
         packed[pl.ds(ROWS, V // GROUP, stride=16), :] = jnp.zeros((V // GROUP, LANES), F32)
-
-    row_id = (rep * (FAR * NEAR) + red) * ROWS + step
-    label = vir_irrep[slab_a[0] * A + row_id // O] ^ occ_irrep[row_id % O]
-    partner = occ ^ label
-    low = jnp.zeros((1, O), jnp.int32)
-    high = jnp.zeros((1, O), jnp.int32)
-    for g in range(8):
-        low = jnp.where(partner == g, starts[g : g + 1, :O], low)
-        high = jnp.where(partner == g, starts[g + 1 : g + 2, :O], high)
-    c_index = lax.broadcasted_iota(jnp.int32, (V, O), 0)
-    kept = (c_index >= low) & (c_index < high)
-    row[:, :O] = jnp.where(kept, amplitudes[0].astype(F32), 0.0)
-    total = jnp.zeros((V // GROUP, LANES), F32)
-    for u in range(GROUP):
-        part = row[pl.ds(u, V // GROUP, stride=GROUP), :]
-        total += jnp.dot(part[:, :O].astype(BF), chosen[u, :O], preferred_element_type=F32)
-    packed[pl.ds(step, V // GROUP, stride=16), :] = total
-
-    @pl.when(step == ROWS - 1)
+        row[...] = jnp.zeros_like(row)
+
+    for j in range(STEP):
+        row_id = (rep * (FAR * NEAR) + red) * ROWS + step * STEP + j
+        label = vir_irrep[slab_a[0] * A + row_id // O] ^ occ_irrep[row_id % O]
+        partner = occ ^ label
+        low = jnp.zeros((1, O), jnp.int32)
+        high = jnp.zeros((1, O), jnp.int32)
+        for g in range(8):
+            low = jnp.where(partner == g, starts[g : g + 1, :O], low)
+            high = jnp.where(partner == g, starts[g + 1 : g + 2, :O], high)
+        c_index = lax.broadcasted_iota(jnp.int32, (V, O), 0)
+        kept = (c_index >= low) & (c_index < high)
+        row[j, :, :O] = jnp.where(kept, amplitudes[j].astype(F32), 0.0)
+    for j in range(STEP):
+        left = jnp.concatenate(
+            [row[j, pl.ds(u, V // GROUP, stride=GROUP), :].astype(BF) for u in range(GROUP)], axis=1
+        )
+        total = jnp.dot(left, chosen[...], preferred_element_type=F32)
+        packed[pl.ds(step * STEP + j, V // GROUP, stride=16), :] = total
+
+    @pl.when(step == ROWS // STEP - 1)
     def _():
         rows = PARTS * 16
         for e in range(NEAR):
@@ -116,52 +122,57 @@
                 out[e, far * rows : (far + 1) * rows] = packed[first : first + rows].astype(BF)
 
 
-def multiply(place, vir_irrep, slab_a, slab_b, occ_row, vir_rows, amps, ints, out, left):
+def multiply(place, vir_irrep, slab_a, slab_b, occ_row, amps, ints, out, left, row_label, total):
     red, rep = place()
-    far_own = red // NEAR
+    step = pl.program_id(0)
     occ = occ_row[...]
+    rows = NEAR * 16
+
+    @pl.when(step == 0)
+    def _():
+        for s in range(NEAR):
+            for block in range(FAR * PARTS):
+                left[s * 16 : (s + 1) * 16, block * LANES : (block + 1) * LANES] = amps[
+                    s, block * 16 : (block + 1) * 16
+                ]
+        row = lax.broadcasted_iota(jnp.int32, (rows, LANES), 0)
+        local = (row // 16) * ROWS + row % 16
+        second = local >= O
+        i_index = jnp.where(second, local - O, local)
+        i_label = jnp.zeros((rows, LANES), jnp.int32)
+        for g in range(1, 8):
+            start = jnp.sum(jnp.where(occ < g, 1.0, 0.0), axis=1, keepdims=True).astype(jnp.int32)
+            i_label += jnp.where(i_index >= start, 1, 0)
+        a_first = slab_a[0] * A + (rep * FAR + red // NEAR) * 2
+        row_label[...] = i_label ^ jnp.where(second, vir_irrep[a_first + 1], vir_irrep[a_first])
+        total[...] = jnp.zeros_like(total)
+
     _, _, pos_col = positions(occ)
-    rows = NEAR * 16
-    for s in range(NEAR):
-        for block in range(FAR * PARTS):
-            left[s * 16 : (s + 1) * 16, block * LANES : (block + 1) * LANES] = amps[
-                s, block * 16 : (block + 1) * 16
-            ]
-    row = lax.broadcasted_iota(jnp.int32, (rows, 1), 0)
-    local = (row // 16) * ROWS + row % 16
-    second = local >= O
-    i_index = jnp.where(second, local - O, local)
-    i_label = jnp.zeros((rows, 1), jnp.int32)
-    for g in range(1, 8):
-        start = jnp.sum(jnp.where(occ < g, 1.0, 0.0), axis=1, keepdims=True).astype(jnp.int32)
-        i_label += jnp.where(i_index >= start, 1, 0)
-    a_first = slab_a[0] * A + (rep * FAR + far_own) * 2
-    row_label = i_label ^ jnp.where(second, vir_irrep[a_first + 1], vir_irrep[a_first])
-    lane = lax.broadcasted_iota(jnp.int32, (O, LANES), 1)
-    main = jnp.zeros((rows, LANES), F32)
-    rest = jnp.zeros((rows, LANES), F32)
-    amounts = left[...]
-    for pair in range(B // 2):
-        right = jnp.concatenate([ints[2 * pair], ints[2 * pair + 1]], axis=1)
-        both = jnp.dot(amounts, right, preferred_element_type=F32)
-        for half in range(2):
-            b = 2 * pair + half
-            b_label = vir_irrep[slab_b[0] * B + b]
-            part = both[:, half * LANES : half * LANES + O]
-            part = jnp.where((row_label ^ b_label) == occ, part, 0.0)
-            pieces = thirds(part)
-            if SLOTS * b < LANES:
-                pick = jnp.where(lane == pos_col + SLOTS * b, 1.0, 0.0).astype(BF)
-                for piece in pieces:
-                    main += jnp.dot(piece, pick, preferred_element_type=F32)
-            if SLOTS * (b + 1) > LANES:
-                pick = jnp.where(lane == pos_col + (SLOTS * b - LANES), 1.0, 0.0).astype(BF)
-                for piece in pieces:
-                    rest += jnp.dot(piece, pick, preferred_element_type=F32)
-    moved = pltpu.roll(rest, LANES // 2, 1)
-    for e in range(NEAR):
-        out[e, :16] = main[e * 16 : (e + 1) * 16]
-        out[e, 16:] = rest[e * 16 : e * 16 + 8] + moved[e * 16 + 8 : e * 16 + 16]
+    pad = jnp.full((1, LANES - O), 64, jnp.int32)
+    occ_lanes = jnp.concatenate([occ, pad], axis=1)
+    lane = lax.broadcasted_iota(jnp.int32, (O, 2 * LANES), 1)
+    right = jnp.concatenate([ints[0], ints[1]], axis=1)
+    both = jnp.dot(left[...], right, preferred_element_type=F32)
+    for half in range(2):
+        b = 2 * step + half
+        b_label = vir_irrep[slab_b[0] * B + b]
+        part = both[:, half * LANES : (half + 1) * LANES]
+        part = jnp.where((row_label[...] ^ b_label) == occ_lanes, part, 0.0)
+        pick = jnp.where(lane == pos_col + SLOTS * b, 1.0, 0.0)
+        pick = jnp.concatenate([pick, jnp.zeros((LANES - O, 2 * LANES), F32)], axis=0).astype(BF)
+        total[...] += jnp.dot(
+            jnp.concatenate(thirds(part), axis=1),
+            jnp.concatenate([pick] * 3, axis=0),
+            preferred_element_type=F32,
+        )
+
+    @pl.when(step == B // 2 - 1)
+    def _():
+        rest = total[:, LANES:]
+        moved = pltpu.roll(rest, LANES // 2, 1)
+        for e in range(NEAR):
+            out[e, :16] = total[e * 16 : (e + 1) * 16, :LANES]
+            out[e, 16:] = rest[e * 16 : e * 16 + 8] + moved[e * 16 + 8 : e * 16 + 16]
 
 
 def finish(
@@ -233,18 +244,24 @@
     )(vir_irrep, slab_b, occ_row, integrals)
 
 
+def fixed(shape):
+    return pl.BlockSpec(shape, lambda step: (0,) * len(shape))
+
+
 def call_pack_amplitudes(place, vir_irrep, occ_irrep, slab_a, occ_row, vir_rows, amplitudes, **kw):
-    fixed = lambda shape: pl.BlockSpec(shape, lambda r: (0,) * len(shape))
     return pl.pallas_call(
         functools.partial(pack_amplitudes, place),
-        out_shape=jax.ShapeDtypeStruct((NEAR, FAR * PARTS * 16, LANES), BF),
-        grid=(ROWS,),
-        in_specs=[SMEM, SMEM, SMEM, fixed((1, O)), fixed((B, O)), pl.BlockSpec((1, V, O), lambda r: (r, 0, 0))],
-        out_specs=fixed((NEAR, FAR * PARTS * 16, LANES)),
+        out_shape=(
+            jax.ShapeDtypeStruct((NEAR, FAR * PARTS * 16, LANES), BF),
+            jax.ShapeDtypeStruct((1, 1), jnp.int32),
+        ),
+        grid=(ROWS // STEP,),
+        in_specs=[SMEM, SMEM, SMEM, fixed((1, O)), fixed((B, O)), pl.BlockSpec((STEP, V, O), lambda r: (r, 0, 0))],
+        out_specs=(fixed((NEAR, FAR * PARTS * 16, LANES)), SMEM),
         scratch_shapes=[
             pltpu.VMEM((16, LANES), jnp.int32),
-            pltpu.VMEM((GROUP, LANES, LANES), BF),
-            pltpu.VMEM((V, LANES), F32),
+            pltpu.VMEM((GROUP * LANES, LANES), BF),
+            pltpu.VMEM((STEP, V, LANES), F32),
             pltpu.VMEM((V // GROUP * 16, LANES), F32),
         ],
         compiler_params=params(32),
@@ -254,17 +271,26 @@
     )(vir_irrep, occ_irrep, slab_a, occ_row, vir_rows, amplitudes)
 
 
-def call_multiply(place, vir_irrep, slab_a, slab_b, occ_row, vir_rows, amps, ints, **kw):
+def call_multiply(place, vir_irrep, slab_a, slab_b, occ_row, amps, ints, **kw):
+    depth = FAR * PARTS * LANES
     return pl.pallas_call(
         functools.partial(multiply, place),
         out_shape=jax.ShapeDtypeStruct((NEAR, 24, LANES), F32),
-        in_specs=[SMEM, SMEM, SMEM, VMEM, VMEM, VMEM, VMEM],
-        out_specs=VMEM,
-        scratch_shapes=[pltpu.VMEM((NEAR * 16, FAR * PARTS * LANES), BF)],
-        compiler_params=params(48),
+        grid=(B // 2,),
+        in_specs=[
+            SMEM, SMEM, SMEM, fixed((1, O)), fixed((NEAR, FAR * PARTS * 16, LANES)),
+            pl.BlockSpec((2, depth, LANES), lambda step: (step, 0, 0)),
+        ],
+        out_specs=fixed((NEAR, 24, LANES)),
+        scratch_shapes=[
+            pltpu.VMEM((NEAR * 16, depth), BF),
+            pltpu.VMEM((NEAR * 16, LANES), jnp.int32),
+            pltpu.VMEM((NEAR * 16, 2 * LANES), F32),
+        ],
+        compiler_params=params(60),
         name="multiply",
         **kw,
-    )(vir_irrep, slab_a, slab_b, occ_row, vir_rows, amps, ints)
+    )(vir_irrep, slab_a, slab_b, occ_row, amps, ints)
 
 
 def call_finish(place, vir_irrep, occ_irrep, slab_a, slab_b, occ_energy, vir_energy, occ_row, energy_row, parts, other, **kw):
@@ -278,22 +304,6 @@
         name="finish",
         **kw,
     )(vir_irrep, occ_irrep, slab_a, slab_b, occ_energy, vir_energy, occ_row, energy_row, parts, other)
-
-
-def packed_form(amplitudes, integrals, other_terms, occ_energy, vir_energy, occ_irrep, vir_irrep, slab_a, slab_b):
-    occ_row = occ_irrep.reshape(1, O)
-    vir_rows = vir_irrep.reshape(B, O)
-    ints = call_pack_integrals(own_place, vir_irrep, slab_b, occ_row, integrals.reshape(ROWS, O, O))
-    ints = lax.all_gather(ints, "far", axis=0, tiled=True)
-    ints = lax.all_gather(ints, "rep", axis=0)
-    amps = call_pack_amplitudes(own_place, vir_irrep, occ_irrep, slab_a, occ_row, vir_rows, amplitudes)
-    amps = lax.all_to_all(amps, "near", 0, 0, tiled=True)
-    parts = call_multiply(own_place, vir_irrep, slab_a, slab_b, occ_row, vir_rows, amps, ints)
-    parts = lax.all_to_all(parts, "near", 0, 0, tiled=True)
-    return call_finish(
-        own_place, vir_irrep, occ_irrep, slab_a, slab_b, occ_energy, vir_energy,
-        occ_row, occ_energy.reshape(1, O), parts, other_terms,
-    )
 
 
 def whole_form(amplitudes, integrals, other_terms, occ_energy, vir_energy, occ_irrep, vir_irrep, slab_a, slab_b):
@@ -336,10 +346,30 @@
     return jnp.where(allowed, updated, jnp.zeros_like(updated))
 
 
-def on_device(*args):
-    occ_irrep = args[5]
-    crowded = jnp.any(occ_irrep[SLOTS:] == occ_irrep[:-SLOTS])
-    return lax.cond(crowded, whole_form, packed_form, *args)
+def on_device(
+    amplitudes, integrals, other_terms, occ_energy, vir_energy, occ_irrep, vir_irrep, slab_a, slab_b
+):
+    occ_row = occ_irrep.reshape(1, O)
+    vir_rows = vir_irrep.reshape(B, O)
+    ints = call_pack_integrals(own_place, vir_irrep, slab_b, occ_row, integrals.reshape(ROWS, O, O))
+    ints = lax.all_gather(ints, "far", axis=0, tiled=True)
+    ints = lax.all_gather(ints, "rep", axis=0)
+    amps, most = call_pack_amplitudes(own_place, vir_irrep, occ_irrep, slab_a, occ_row, vir_rows, amplitudes)
+    amps = lax.all_to_all(amps, "near", 0, 0, tiled=True)
+    parts = call_multiply(own_place, vir_irrep, slab_a, slab_b, occ_row, amps, ints)
+    parts = lax.all_to_all(parts, "near", 0, 0, tiled=True)
+
+    def packed_form(amplitudes, integrals, *rest):
+        other_terms, occ_energy, vir_energy, occ_irrep, vir_irrep, slab_a, slab_b, parts = rest
+        return call_finish(
+            own_place, vir_irrep, occ_irrep, slab_a, slab_b, occ_energy, vir_energy,
+            occ_irrep.reshape(1, O), occ_energy.reshape(1, O), parts, other_terms,
+        )
+
+    return lax.cond(
+        most[0, 0] >= SLOTS, lambda *args: whole_form(*args[:-1]), packed_form,
+        amplitudes, integrals, other_terms, occ_energy, vir_energy, occ_irrep, vir_irrep, slab_a, slab_b, parts,
+    )
 
 
 def solution(mesh):

time: 109 us -> 105 us (0.963)
  blocking collectives: 68.4 us -> 55.1 us
  waiting for transfers between devices: 0.02 us -> 9.39 us
  starting transfers between devices: 0.04 us -> 6.08 us
  Pallas kernels: 20.7 us -> 15.9 us
  local copies, waits for them, and re-layouts: 3.3 us -> 1.42 us
  between operations: 14 us -> 15.5 us
  other arithmetic: 1.44 us -> 0 us
    all_to_all x2 -> x1, blocking collectives: 37.7 us -> 24.4 us  [on_device(): amps = lax.all_to_all(amps, 'near', 0, 0, tiled=True)]
    all_to_all x0 -> x1, waiting for transfers between devices: none -> 9.37 us  [on_device(): parts = lax.all_to_all(parts, 'near', 0, 0, tiled=True)]
    all_to_all x0 -> x1, starting transfers between devices: none -> 6.07 us  [on_device(): parts = lax.all_to_all(parts, 'near', 0, 0, tiled=True)]
    pallas_call x1, Pallas kernels: 12 us -> 5.97 us  [call_pack_amplitudes(): pl.pallas_call(functools.partial(pack_amplitudes, place), out_shape=(jax....]
    cond x12 -> x0, local copies, waits for them, and re-layouts: 1.92 us -> none
    pallas_call x1, Pallas kernels: 4.38 us -> 6.17 us  [call_multiply(): pl.pallas_call(functools.partial(multiply, place), out_shape=jax.ShapeDty...]
    reduce_or x1 -> x0, other arithmetic: 1.44 us -> none  [on_device(): crowded = jnp.any(occ_irrep[SLOTS:] == occ_irrep[:-SLOTS])]
  transfers between devices with their start and end apart: 1 -> 2, of which waited for: 0 -> 1; matrix products, arithmetic and copies ran while one was open for 1% -> 1% of each run, Pallas kernels for 11% -> 6%
where the time goes in v2:
time: 105 us; the launch traced here: 104 us
  blocking collectives  55.1 us (52%)
  Pallas kernels  15.9 us (15%)
  between operations  15.5 us (15%)
  waiting for transfers between devices  9.39 us (9%)
  starting transfers between devices  6.08 us (6%)
  local copies, waits for them, and re-layouts  1.42 us (1%)
    all_gather x1, blocking collectives, on_device(): ints = lax.all_gather(ints, 'far', axis=0, tiled=True)  30.7 us
    all_to_all x1, blocking collectives, on_device(): amps = lax.all_to_all(amps, 'near', 0, 0, tiled=True)  24.4 us
    all_to_all x1, waiting for transfers between devices, on_device(): parts = lax.all_to_all(parts, 'near', 0, 0, tiled=True)  9.37 us
    pallas_call x1, Pallas kernels, call_multiply(): pl.pallas_call(functools.partial(multiply, place), out_shape=jax.ShapeDty...  6.17 us
    all_to_all x1, starting transfers between devices, on_device(): parts = lax.all_to_all(parts, 'near', 0, 0, tiled=True)  6.07 us
    pallas_call x1, Pallas kernels, call_pack_amplitudes(): pl.pallas_call(functools.partial(pack_amplitudes, place), out_shape=(jax....  5.97 us
    pallas_call x1, Pallas kernels, call_finish(): pl.pallas_call(functools.partial(finish, place), out_shape=jax.ShapeDtype...  2.34 us
  transfers between devices with their start and end apart: 2, of which 1 were waited for; matrix products, arithmetic and copies ran while one was open for 1% of the time, Pallas kernels for 6%

profile of v2, /device:TPU:6, one launch (start us, length us, event | category | flops | bytes accessed | tf_op | source)
XLA Modules:
  0.0 103.5 jit_solution(14876571203816648549)
XLA Ops:
  6.5 0.0 copy-start
  6.5 0.0 copy-start.2
  6.5 0.0 all-gather.6.cloned.1.call-start
  7.2 1.4 %pack_integrals.1 = bf16[384,128]{1,0:T(8,128)(2,1)S(1)} custom-call(s32[960]{0:T(1024)} %vir_irrep.5, s32[1]{0:T(128)S(6)} %copy.51.slab_b, s32[1,120]{1,0:T(1,128)} %bitcast.30, bf16[15,120,120]{2,1,0:T(8,128)(2,1)} %bitcast.37), custom_call_target="tpu_custom_call" | custom-call | flops 20000000 | bytes 600000 | tf_op jit(solution)/shard_map/pack_integrals/pallas_call | solution.py:234
  8.6 30.7 %all_gather.12 = bf16[1536,128]{1,0:T(8,128)(2,1)} all-gather(bf16[384,128]{1,0:T(8,128)(2,1)S(1)} %pack_integrals.1), channel_id=1, replica_groups=mesh['far'=4,'near'=16,'rep'=8] {'far'}, dimensions={0}, use_global_device_ids=true | all-gather | bytes 491520 | tf_op jit(solution)/shard_map/all_gather | solution.py:355
  39.3 0.0 all-gather.6.cloned.1.call-update
  39.3 0.8 reshape.197.vir_rows
  40.7 6.0 %pack_amplitudes.1 = (bf16[16,192,128]{2,1,0:T(8,128)(2,1)S(1)}, s32[1,1]{1,0:T(1,128)}) custom-call(s32[960]{0:T(1024)} %vir_irrep.5, s32[120]{0:T(128)} %occ_irrep.1, s32[1]{0:T(128)S(6)} %copy.50.slab_a, s32[1,120]{1,0:T(1,128)} %bitcast.31, s32[8,120]{1,0:T(8,128)S(1)} %reshape.197.vir_rows, bf16[15,960,120]{2,1,0:T(8,128)(2,1)} %amplitudes.1), custom_call_target="tpu_custom_call" | custom-call | flops 1000000000 | bytes 4500000 | tf_op jit(solution)/shard_map/pack_amplitudes/pallas_call | solution.py:252
  46.7 0.0 copy-start.1
  46.7 0.0 copy-start.3
  46.7 0.0 copy-start.4
  46.8 0.0 copy-start.5
  46.8 24.4 %all_to_all.22.amps = bf16[16,192,128]{2,1,0:T(8,128)(2,1)} all-to-all(bf16[16,192,128]{2,1,0:T(8,128)(2,1)S(1)} %get-tuple-element.62), channel_id=1, replica_groups=mesh['far'=4,'near'=16,'rep'=8] {'near'}, dimensions={0} | all-to-all | bytes 1572864 | tf_op jit(solution)/shard_map/all_to_all | solution.py:358
  71.2 0.0 all-gather.6.cloned.1.call-done
  71.2 0.0 copy-done
  71.2 0.0 copy-done.2
  71.2 6.2 %multiply.3 = f32[16,24,128]{2,1,0:T(8,128)} custom-call(s32[960]{0:T(1024)S(1)} %copy-done.2, s32[1]{0:T(128)S(6)} %copy.50.slab_a, s32[1]{0:T(128)S(6)} %copy.51.slab_b, s32[1,120]{1,0:T(1,128)S(1)} %bitcast.32, bf16[16,192,128]{2,1,0:T(8,128)(2,1)} %all_to_all.22.amps, bf16[8,1536,128]{2,1,0:T(8,128)(2,1)} %bitcast.35), custom_call_target="tpu_custom_call" | custom-call | tf_op jit(solution)/shard_map/multiply/pallas_call | solution.py:276
  77.3 6.1 %all-to-all-start.2 = ((f32[16,24,128]{2,1,0:T(8,128)}), f32[16,24,128]{2,1,0:T(8,128)S(1)}, u32[]{:S(2)}, u32[]{:S(2)}) async-start(f32[16,24,128]{2,1,0:T(8,128)} %multiply.3), calls=%async_computation.2 | async-start | bytes 393216 | tf_op jit(solution)/shard_map/all_to_all | solution.py:360
  84.1 9.4 %all-to-all-done.2 = f32[16,24,128]{2,1,0:T(8,128)S(1)} async-done(((f32[16,24,128]{2,1,0:T(8,128)}), f32[16,24,128]{2,1,0:T(8,128)S(1)}, u32[]{:S(2)}, u32[]{:S(2)}) %all-to-all-start.2) | async-done | bytes 196640 | tf_op jit(solution)/shard_map/all_to_all | solution.py:360
  93.5 0.0 copy-done.1
  93.5 0.0 copy-done.3
  93.5 0.0 copy-done.4
  93.5 0.0 copy-done.5
  93.5 2.6 %conditional.1 = (f32[15,8,120]{2,1,0:T(8,128)S(1)}) conditional(s32[]{:T(128)} %bitcast.14, (s32[120]{0:T(128)S(1)}, f32[120]{0:T(128)S(1)}, s32[960]{0:T(1024)S(1)}, s32[1]{0:T(128)}, s32[1]{0:T(128)}, /*index=5*/f32[960]{0:T(1024)S(1)}, f32[16,24,128]{2,1,0:T(8,128)S(1)}, f32[15,8,120]{2,1,0:T(8,128)S(1)}) %tuple.45, (s32[1]{0:T(128)}, ...), branch_computations={%region_0.0_spmd, %region_1.3_spmd} | conditional | flops 3319191552 | bytes 92437360 | solution.py:369
  93.5 2.3 %finish.1 = f32[15,8,120]{2,1,0:T(8,128)S(1)} custom-call(s32[960]{0:T(1024)S(1)} %get-tuple-element.42.vir_irrep, s32[120]{0:T(128)S(1)} %get-tuple-element.43.occ_irrep, s32[1]{0:T(128)} %get-tuple-element.44.slab_a, s32[1]{0:T(128)} %get-tuple-element.45.slab_b, f32[120]{0:T(128)S(1)} %get-tuple-element.46.occ_energy, ...), custom_call_target="tpu_custom_call" | custom-call | tf_op jit(solution)/shard_map/cond/branch_0_fun/finish/pallas_call | solution.py:297
  96.1 0.0 copy-start.6
  96.1 0.6 copy-done.6
Async XLA Ops:
  6.5 64.6 %copy-start = (s32[120]{0:T(128)S(1)}, s32[120]{0:T(128)}, u32[]{:S(2)}) copy-start(s32[120]{0:T(128)} %occ_irrep.1) | copy-start | bytes 1444
  6.5 64.6 %copy-start.2 = (s32[960]{0:T(1024)S(1)}, s32[960]{0:T(1024)}, u32[]{:S(2)}) copy-start(s32[960]{0:T(1024)} %vir_irrep.5) | copy-start | bytes 11524
  6.5 64.6 %all-gather.6.cloned.1.call-start = ((), (), s32[]{:S(2)}) async-start(), calls=%async_computation.5 | async-start | bytes 3538944 | tf_op jit(solution)/shard_map/all_gather | solution.py:356
  46.7 46.7 %copy-start.1 = (f32[120]{0:T(128)S(1)}, f32[120]{0:T(128)}, u32[]{:S(2)}) copy-start(f32[120]{0:T(128)} %param.14) | copy-start | bytes 1444
  46.7 46.7 %copy-start.3 = (f32[960]{0:T(1024)S(1)}, f32[960]{0:T(1024)}, u32[]{:S(2)}) copy-start(f32[960]{0:T(1024)} %param.15) | copy-start | bytes 11524
  46.7 46.7 %copy-start.4 = (bf16[15,120,1,120]{3,1,2,0:T(8,128)(2,1)S(1)}, bf16[15,120,1,120]{3,1,2,0:T(8,128)(2,1)}, u32[]{:S(2)}) copy-start(bf16[15,120,1,120]{3,1,2,0:T(8,128)(2,1)} %param.12) | copy-start | bytes 1296004
  46.8 46.7 %copy-start.5 = (f32[15,8,120]{2,1,0:T(8,128)S(1)}, f32[15,8,120]{2,1,0:T(8,128)}, u32[]{:S(2)}) copy-start(f32[15,8,120]{2,1,0:T(8,128)} %param.13) | copy-start | bytes 172804
  77.3 16.1 %all-to-all-start.2 = ((f32[16,24,128]{2,1,0:T(8,128)}), f32[16,24,128]{2,1,0:T(8,128)S(1)}, u32[]{:S(2)}, u32[]{:S(2)}) async-start(f32[16,24,128]{2,1,0:T(8,128)} %multiply.3), calls=%async_computation.2 | async-start | bytes 393216 | tf_op jit(solution)/shard_map/all_to_all | solution.py:360
  96.1 0.6 copy-start.6
Sparse Core Ops, SparseCore 0:
  39.4 30.4 all-gather.5

commit v3 on v2

--- a/solution.py
+++ b/solution.py
@@ -66,7 +66,9 @@
         kept = jnp.where((occ_col ^ label) == occ, integrals[c].astype(F32), 0.0).astype(BF)
         first = LANES * (c // GROUP) + SLOTS * (c % GROUP)
         scratch[first : first + SLOTS, :O] = jnp.dot(pick, kept, preferred_element_type=F32)
-    out[...] = scratch[...].astype(BF)
+    packed = scratch[...].astype(BF)
+    for far in range(FAR):
+        out[far] = packed
 
 
 def pack_amplitudes(
@@ -122,57 +124,58 @@
                 out[e, far * rows : (far + 1) * rows] = packed[first : first + rows].astype(BF)
 
 
-def multiply(place, vir_irrep, slab_a, slab_b, occ_row, amps, ints, out, left, row_label, total):
+def slot_owner(place, slot):
+    _, rep = place()
+    return ((rep // 2 + (REP // 2 - slot // 2)) % (REP // 2)) * 2 + (rep + slot) % 2
+
+
+def multiply(place, vir_irrep, slab_a, slab_b, occ_row, amps, *rest):
+    ints, (out, left, held, sems) = rest[:REP], rest[REP:]
     red, rep = place()
-    step = pl.program_id(0)
+    copies = [pltpu.make_async_copy(ints[slot], held.at[slot], sems.at[slot]) for slot in range(REP)]
+    for copy in copies:
+        copy.start()
     occ = occ_row[...]
     rows = NEAR * 16
-
-    @pl.when(step == 0)
-    def _():
-        for s in range(NEAR):
-            for block in range(FAR * PARTS):
-                left[s * 16 : (s + 1) * 16, block * LANES : (block + 1) * LANES] = amps[
-                    s, block * 16 : (block + 1) * 16
-                ]
-        row = lax.broadcasted_iota(jnp.int32, (rows, LANES), 0)
-        local = (row // 16) * ROWS + row % 16
-        second = local >= O
-        i_index = jnp.where(second, local - O, local)
-        i_label = jnp.zeros((rows, LANES), jnp.int32)
-        for g in range(1, 8):
-            start = jnp.sum(jnp.where(occ < g, 1.0, 0.0), axis=1, keepdims=True).astype(jnp.int32)
-            i_label += jnp.where(i_index >= start, 1, 0)
-        a_first = slab_a[0] * A + (rep * FAR + red // NEAR) * 2
-        row_label[...] = i_label ^ jnp.where(second, vir_irrep[a_first + 1], vir_irrep[a_first])
-        total[...] = jnp.zeros_like(total)
-
+    for s in range(NEAR):
+        for block in range(FAR * PARTS):
+            left[s * 16 : (s + 1) * 16, block * LANES : (block + 1) * LANES] = amps[
+                s, block * 16 : (block + 1) * 16
+            ]
     _, _, pos_col = positions(occ)
-    pad = jnp.full((1, LANES - O), 64, jnp.int32)
-    occ_lanes = jnp.concatenate([occ, pad], axis=1)
-    lane = lax.broadcasted_iota(jnp.int32, (O, 2 * LANES), 1)
-    right = jnp.concatenate([ints[0], ints[1]], axis=1)
-    both = jnp.dot(left[...], right, preferred_element_type=F32)
-    for half in range(2):
-        b = 2 * step + half
-        b_label = vir_irrep[slab_b[0] * B + b]
-        part = both[:, half * LANES : (half + 1) * LANES]
-        part = jnp.where((row_label[...] ^ b_label) == occ_lanes, part, 0.0)
-        pick = jnp.where(lane == pos_col + SLOTS * b, 1.0, 0.0)
-        pick = jnp.concatenate([pick, jnp.zeros((LANES - O, 2 * LANES), F32)], axis=0).astype(BF)
-        total[...] += jnp.dot(
-            jnp.concatenate(thirds(part), axis=1),
-            jnp.concatenate([pick] * 3, axis=0),
-            preferred_element_type=F32,
-        )
-
-    @pl.when(step == B // 2 - 1)
-    def _():
-        rest = total[:, LANES:]
-        moved = pltpu.roll(rest, LANES // 2, 1)
-        for e in range(NEAR):
-            out[e, :16] = total[e * 16 : (e + 1) * 16, :LANES]
-            out[e, 16:] = rest[e * 16 : e * 16 + 8] + moved[e * 16 + 8 : e * 16 + 16]
+    occ_lanes = jnp.concatenate([occ, jnp.full((1, LANES - O), 64, jnp.int32)], axis=1)
+    pos_lanes = jnp.concatenate([pos_col, jnp.full((LANES - O, 1), -4 * LANES, jnp.int32)], axis=0)
+    row = lax.broadcasted_iota(jnp.int32, (rows, LANES), 0)
+    local = (row // 16) * ROWS + row % 16
+    second = local >= O
+    i_index = jnp.where(second, local - O, local)
+    i_label = jnp.zeros((rows, LANES), jnp.int32)
+    for g in range(1, 8):
+        start = jnp.sum(jnp.where(occ < g, 1.0, 0.0), axis=1, keepdims=True).astype(jnp.int32)
+        i_label += jnp.where(i_index >= start, 1, 0)
+    a_first = slab_a[0] * A + (rep * FAR + red // NEAR) * 2
+    row_label = i_label ^ jnp.where(second, vir_irrep[a_first + 1], vir_irrep[a_first])
+    wanted = row_label ^ occ_lanes
+    lane = lax.broadcasted_iota(jnp.int32, (LANES, 2 * LANES), 1)
+    total = jnp.zeros((rows, 2 * LANES), F32)
+    for pair in range(REP // 2):
+        copies[2 * pair].wait()
+        copies[2 * pair + 1].wait()
+        right = jnp.concatenate([held[2 * pair], held[2 * pair + 1]], axis=1)
+        both = jnp.dot(left[...], right, preferred_element_type=F32)
+        for half in range(2):
+            slot = 2 * pair + half
+            b_label = vir_irrep[slab_b[0] * B + slot_owner(place, slot)]
+            part = both[:, half * LANES : (half + 1) * LANES]
+            part = jnp.where(wanted == b_label, part, 0.0)
+            pick = jnp.where(lane == pos_lanes + SLOTS * slot, 1.0, 0.0).astype(BF)
+            for piece in thirds(part):
+                total += jnp.dot(piece, pick, preferred_element_type=F32)
+    rest = total[:, LANES:]
+    moved = pltpu.roll(rest, LANES // 2, 1)
+    for e in range(NEAR):
+        out[e, :16] = total[e * 16 : (e + 1) * 16, :LANES]
+        out[e, 16:] = rest[e * 16 : e * 16 + 8] + moved[e * 16 + 8 : e * 16 + 16]
 
 
 def finish(
@@ -189,16 +192,16 @@
     mains = jnp.concatenate(thirds(main), axis=0)
     rests = jnp.concatenate(thirds(rest), axis=0)
     lane = lax.broadcasted_iota(jnp.int32, (LANES, O), 0)
-    for b in range(B):
+    for slot in range(REP):
         value = jnp.zeros((48, O), F32)
-        if SLOTS * b < LANES:
-            pick = jnp.where(lane == pos_row + SLOTS * b, 1.0, 0.0).astype(BF)
+        if SLOTS * slot < LANES:
+            pick = jnp.where(lane == pos_row + SLOTS * slot, 1.0, 0.0).astype(BF)
             value += jnp.dot(mains, pick, preferred_element_type=F32)
-        if SLOTS * (b + 1) > LANES:
-            at = pos_row + (SLOTS * b - LANES)
+        if SLOTS * (slot + 1) > LANES:
+            at = pos_row + (SLOTS * slot - LANES)
             pick = jnp.where((lane == at) & (lane < LANES // 2), 1.0, 0.0).astype(BF)
             value += jnp.dot(rests, pick, preferred_element_type=F32)
-        cycle[pl.ds(b, 16, stride=B), :O] = (value[:16] + value[16:32]) + value[32:]
+        cycle[pl.ds(slot_owner(place, slot), 16, stride=B), :O] = (value[:16] + value[16:32]) + value[32:]
     b_first = slab_b[0] * B
     b_index = lax.broadcasted_iota(jnp.int32, (B, 1), 0)
     b_label = jnp.zeros((B, 1), jnp.int32)
@@ -219,7 +222,10 @@
 
 
 def own_place():
-    return lax.axis_index("far") * NEAR + lax.axis_index("near"), lax.axis_index("rep")
+    return (
+        lax.axis_index("far") * NEAR + lax.axis_index("near"),
+        lax.axis_index("x") * 2 + lax.axis_index("core"),
+    )
 
 
 SMEM = pl.BlockSpec(memory_space=pltpu.SMEM)
@@ -233,7 +239,7 @@
 def call_pack_integrals(place, vir_irrep, slab_b, occ_row, integrals, **kw):
     return pl.pallas_call(
         functools.partial(pack_integrals, place),
-        out_shape=jax.ShapeDtypeStruct((PARTS * LANES, LANES), BF),
+        out_shape=jax.ShapeDtypeStruct((FAR, PARTS * LANES, LANES), BF),
         in_specs=[SMEM, SMEM, VMEM, VMEM],
         out_specs=VMEM,
         scratch_shapes=[pltpu.VMEM((PARTS * LANES, LANES), F32)],
@@ -276,21 +282,17 @@
     return pl.pallas_call(
         functools.partial(multiply, place),
         out_shape=jax.ShapeDtypeStruct((NEAR, 24, LANES), F32),
-        grid=(B // 2,),
-        in_specs=[
-            SMEM, SMEM, SMEM, fixed((1, O)), fixed((NEAR, FAR * PARTS * 16, LANES)),
-            pl.BlockSpec((2, depth, LANES), lambda step: (step, 0, 0)),
-        ],
-        out_specs=fixed((NEAR, 24, LANES)),
+        in_specs=[SMEM, SMEM, SMEM, VMEM, VMEM] + [pl.BlockSpec(memory_space=pl.ANY)] * REP,
+        out_specs=VMEM,
         scratch_shapes=[
             pltpu.VMEM((NEAR * 16, depth), BF),
-            pltpu.VMEM((NEAR * 16, LANES), jnp.int32),
-            pltpu.VMEM((NEAR * 16, 2 * LANES), F32),
+            pltpu.VMEM((REP, depth, LANES), BF),
+            pltpu.SemaphoreType.DMA((REP,)),
         ],
-        compiler_params=params(60),
+        compiler_params=params(32),
         name="multiply",
         **kw,
-    )(vir_irrep, slab_a, slab_b, occ_row, amps, ints)
+    )(vir_irrep, slab_a, slab_b, occ_row, amps, *ints)
 
 
 def call_finish(place, vir_irrep, occ_irrep, slab_a, slab_b, occ_energy, vir_energy, occ_row, energy_row, parts, other, **kw):
@@ -307,36 +309,30 @@
 
 
 def whole_form(amplitudes, integrals, other_terms, occ_energy, vir_energy, occ_irrep, vir_irrep, slab_a, slab_b):
-    red = ("far", "near")
+    red, rep = ("far", "near"), ("x", "core")
     red_count = FAR * NEAR
-    rows_dev = amplitudes.shape[0]
-    vir_local = integrals.shape[0]
-    b_local = integrals.shape[2]
-    occupied = occ_energy.shape[0]
+    red_index, rep_index = own_place()
     a_start = slab_a[0] * A
     b_start = slab_b[0] * B
     b_labels = lax.dynamic_slice_in_dim(vir_irrep, b_start, B)
     b_energy = lax.dynamic_slice_in_dim(vir_energy, b_start, B)
-    c_labels = lax.dynamic_slice_in_dim(vir_irrep, lax.axis_index(red) * vir_local, vir_local)
+    c_labels = lax.dynamic_slice_in_dim(vir_irrep, red_index * ROWS, ROWS)
     pair_ck = pair_labels(c_labels, occ_irrep)
     pair_bj = pair_labels(b_labels, occ_irrep)
-    own_pairs = lax.dynamic_slice_in_dim(pair_bj, lax.axis_index("rep") * b_local, b_local, 0)
-    local_kept = (pair_ck[:, :, None, None] == own_pairs[None, None]).astype(jnp.bfloat16)
-    gathered = lax.all_gather(integrals * local_kept, "rep", axis=2, tiled=True)
+    own_pairs = lax.dynamic_slice_in_dim(pair_bj, rep_index, 1, 0)
+    local_kept = (pair_ck[:, :, None, None] == own_pairs[None, None]).astype(BF)
+    kept = (integrals * local_kept).reshape(1, ROWS * O, O)
+    gathered = lax.all_to_all(jnp.broadcast_to(kept, (REP, ROWS * O, O)), rep, 0, 0, tiled=True)
     exchanged = lax.all_to_all(amplitudes, red, split_axis=1, concat_axis=0, tiled=True)
-    flat_amps = exchanged.reshape(exchanged.shape[0], vir_local * occupied)
-    flat_ints = gathered.reshape(vir_local * occupied, B * occupied)
-    mine = lax.psum_scatter(
-        jnp.dot(flat_amps, flat_ints, preferred_element_type=jnp.float32),
-        red,
-        scatter_dimension=0,
-        tiled=True,
-    )
-    cycle_term = mine.reshape(rows_dev, B, occupied)
-    first_global = (lax.axis_index("rep") * red_count + lax.axis_index(red)) * rows_dev
-    row_ids = first_global + jnp.arange(rows_dev, dtype=jnp.int32)
-    a_index = a_start + row_ids // occupied
-    i_index = row_ids % occupied
+    flat_amps = exchanged.reshape(red_count * ROWS, ROWS * O)
+    flat_ints = jnp.swapaxes(gathered, 0, 1).reshape(ROWS * O, B * O)
+    parts = jnp.dot(flat_amps, flat_ints, preferred_element_type=F32).reshape(red_count, ROWS, B * O)
+    mine = jnp.sum(lax.all_to_all(parts, red, 0, 0, tiled=True), axis=0)
+    cycle_term = mine.reshape(ROWS, B, O)
+    first_global = (rep_index * red_count + red_index) * ROWS
+    row_ids = first_global + jnp.arange(ROWS, dtype=jnp.int32)
+    a_index = a_start + row_ids // O
+    i_index = row_ids % O
     pair_ai = jnp.bitwise_xor(vir_irrep[a_index], occ_irrep[i_index])
     allowed = pair_ai[:, None, None] == pair_bj[None]
     row_energy = occ_energy[i_index] - vir_energy[a_index]
@@ -352,8 +348,10 @@
     occ_row = occ_irrep.reshape(1, O)
     vir_rows = vir_irrep.reshape(B, O)
     ints = call_pack_integrals(own_place, vir_irrep, slab_b, occ_row, integrals.reshape(ROWS, O, O))
-    ints = lax.all_gather(ints, "far", axis=0, tiled=True)
-    ints = lax.all_gather(ints, "rep", axis=0)
+    ints = lax.all_to_all(ints, "far", 0, 0, tiled=True).reshape(FAR * PARTS * LANES, LANES)
+    count = REP // 2
+    held = [ints] + [lax.ppermute(ints, "x", [(i, (i + s) % count) for i in range(count)]) for s in range(1, count)]
+    ints = [half for own in held for half in (own, lax.ppermute(own, "core", [(0, 1), (1, 0)]))]
     amps, most = call_pack_amplitudes(own_place, vir_irrep, occ_irrep, slab_a, occ_row, vir_rows, amplitudes)
     amps = lax.all_to_all(amps, "near", 0, 0, tiled=True)
     parts = call_multiply(own_place, vir_irrep, slab_a, slab_b, occ_row, amps, ints)
@@ -373,11 +371,12 @@
 
 
 def solution(mesh):
-    split = Mesh(mesh.devices.reshape(FAR, NEAR, REP), ("far", "near", "rep"))
+    split = Mesh(mesh.devices.reshape(FAR, NEAR, REP // 2, 2), ("far", "near", "x", "core"))
+    rows = P(("x", "core", "far", "near"), None, None)
     placed = (
-        P(("rep", "far", "near"), None, None),
-        P(("far", "near"), None, "rep", None),
-        P(("rep", "far", "near"), None, None),
+        rows,
+        P(("far", "near"), None, ("x", "core"), None),
+        rows,
         P(),
         P(),
         P(),
@@ -389,6 +388,6 @@
         on_device,
         mesh=split,
         in_specs=placed,
-        out_specs=P(("rep", "far", "near"), None, None),
+        out_specs=rows,
         check_vma=False,
     )

time: 105 us -> 107 us (1.019)
  blocking collectives: 55.1 us -> 0 us
  starting transfers between devices: 6.08 us -> 49 us
  waiting for transfers between devices: 9.39 us -> 32.9 us
  between operations: 15.5 us -> 2.15 us
  Pallas kernels: 15.9 us -> 18 us
  local copies, waits for them, and re-layouts: 1.42 us -> 3.15 us
    all_gather x1 -> x0, blocking collectives: 30.7 us -> none  [on_device(): ints = lax.all_gather(ints, 'far', axis=0, tiled=True)]
    all_to_all x0 -> x2, starting transfers between devices: none -> 25.5 us  [the longest x1 15.1 us: on_device(): lax.all_to_all(ints, 'far', 0, 0, tiled=True)]
    all_to_all x1 -> x0, blocking collectives: 24.4 us -> none  [on_device(): amps = lax.all_to_all(amps, 'near', 0, 0, tiled=True)]
    ppermute x0 -> x7, starting transfers between devices: none -> 16.3 us  [the longest x3 8.63 us: on_device(): lax.ppermute(ints, 'x', [(i, (i + s) % count) for i in range(count)])]
    all_to_all x0 -> x2, waiting for transfers between devices: none -> 13.2 us  [the longest x1 13.2 us: on_device(): lax.all_to_all(ints, 'far', 0, 0, tiled=True)]
    ppermute x0 -> x7, waiting for transfers between devices: none -> 10.4 us  [the longest x3 8.78 us: on_device(): lax.ppermute(ints, 'x', [(i, (i + s) % count) for i in range(count)])]
    unnamed x14, local copies, waits for them, and re-layouts: 0.65 us -> 2.39 us
    all_to_all x1, starting transfers between devices: 6.07 us -> 7.23 us  [on_device(): parts = lax.all_to_all(parts, 'near', 0, 0, tiled=True)]
  transfers between devices with their start and end apart: 2 -> 10, of which waited for: 1 -> 6; matrix products, arithmetic and copies ran while one was open for 1% -> 1% of each run, Pallas kernels for 6% -> 6%
where the time goes in v3:
time: 107 us; the launch traced here: 105 us
  starting transfers between devices  49 us (46%)
  waiting for transfers between devices  32.9 us (31%)
  Pallas kernels  18 us (17%)
  local copies, waits for them, and re-layouts  3.15 us (3%)
  between operations  2.15 us (2%)
    all_to_all x1, starting transfers between devices, on_device(): lax.all_to_all(ints, 'far', 0, 0, tiled=True)  15.1 us
    all_to_all x1, waiting for transfers between devices, on_device(): lax.all_to_all(ints, 'far', 0, 0, tiled=True)  13.2 us
    all_to_all x1, starting transfers between devices, on_device(): amps = lax.all_to_all(amps, 'near', 0, 0, tiled=True)  10.4 us
    all_to_all x1, waiting for transfers between devices, on_device(): parts = lax.all_to_all(parts, 'near', 0, 0, tiled=True)  9.28 us
    ppermute x3, waiting for transfers between devices, on_device(): lax.ppermute(ints, 'x', [(i, (i + s) % count) for i in range(count)])  8.78 us
    ppermute x3, starting transfers between devices, on_device(): lax.ppermute(ints, 'x', [(i, (i + s) % count) for i in range(count)])  8.63 us
    ppermute x4, starting transfers between devices, on_device(): lax.ppermute(own, 'core', [(0, 1), (1, 0)])  7.65 us
    all_to_all x1, starting transfers between devices, on_device(): parts = lax.all_to_all(parts, 'near', 0, 0, tiled=True)  7.23 us
  transfers between devices with their start and end apart: 10, of which 6 were waited for; matrix products, arithmetic and copies ran while one was open for 1% of the time, Pallas kernels for 6%

profile of v3, /device:TPU:6, one launch (start us, length us, event | category | flops | bytes accessed | tf_op | source)
XLA Modules:
  0.0 105.5 jit_solution(12959053324499898739)
XLA Ops:
  0.0 0.0 copy-start.2
  0.0 0.0 copy-start.4
  0.7 2.2 %pack_integrals.1 = bf16[4,384,128]{2,1,0:T(8,128)(2,1)} custom-call(s32[960]{0:T(1024)} %vir_irrep.5, s32[1]{0:T(128)S(6)} %copy.29.slab_b, s32[1,120]{1,0:T(1,128)} %bitcast.33, bf16[15,120,120]{2,1,0:T(8,128)(2,1)} %bitcast.39), custom_call_target="tpu_custom_call" | custom-call | flops 20000000 | bytes 600000 | tf_op jit(solution)/shard_map/pack_integrals/pallas_call | solution.py:240
  2.8 15.1 %all-to-all-start.4 = ((bf16[4,384,128]{2,1,0:T(8,128)(2,1)}), bf16[4,384,128]{2,1,0:T(8,128)(2,1)S(1)}, u32[]{:S(2)}, u32[]{:S(2)}) async-start(bf16[4,384,128]{2,1,0:T(8,128)(2,1)} %pack_integrals.1), calls=%async_computation.4 | async-start | bytes 786432 | tf_op jit(solution)/shard_map/all_to_all | solution.py:351
  17.9 0.8 reshape.205.vir_rows
  19.3 6.4 %pack_amplitudes.1 = (bf16[16,192,128]{2,1,0:T(8,128)(2,1)}, s32[1,1]{1,0:T(1,128)}) custom-call(s32[960]{0:T(1024)} %vir_irrep.5, s32[120]{0:T(128)} %occ_irrep.1, s32[1]{0:T(128)S(6)} %copy.28.slab_a, s32[1,120]{1,0:T(1,128)} %bitcast.34, s32[8,120]{1,0:T(8,128)S(1)} %reshape.205.vir_rows, bf16[15,960,120]{2,1,0:T(8,128)(2,1)} %amplitudes.1), custom_call_target="tpu_custom_call" | custom-call | flops 1000000000 | bytes 4500000 | tf_op jit(solution)/shard_map/pack_amplitudes/pallas_call | solution.py:258
  25.7 0.0 copy-start.3
  25.7 0.0 copy-start.5
  25.7 13.2 %all-to-all-done.4 = bf16[4,384,128]{2,1,0:T(8,128)(2,1)S(1)} async-done(((bf16[4,384,128]{2,1,0:T(8,128)(2,1)}), bf16[4,384,128]{2,1,0:T(8,128)(2,1)S(1)}, u32[]{:S(2)}, u32[]{:S(2)}) %all-to-all-start.4) | async-done | bytes 393248 | tf_op jit(solution)/shard_map/all_to_all | solution.py:351
  38.9 10.4 %all-to-all-start.3 = ((bf16[16,192,128]{2,1,0:T(8,128)(2,1)}), bf16[16,192,128]{2,1,0:T(8,128)(2,1)S(1)}, u32[]{:S(2)}, u32[]{:S(2)}) async-start(bf16[16,192,128]{2,1,0:T(8,128)(2,1)} %get-tuple-element.62), calls=%async_computation.3 | async-start | bytes 1572864 | tf_op jit(solution)/shard_map/all_to_all | solution.py:356
  49.3 2.4 %collective-permute-start.1 = (bf16[1536,128]{1,0:T(8,128)(2,1)S(1)}, bf16[1536,128]{1,0:T(8,128)(2,1)S(1)}, u32[]{:S(2)}, u32[]{:S(2)}) collective-permute-start(bf16[1536,128]{1,0:T(8,128)(2,1)S(1)} %bitcast.28), channel_id=1, source_target_pairs={{0,2},{2,4},{4,6},{6,0},{1,3},{3,5},{5,7},{7,1},{8,10},{10,12},{12... | collective-permute-start | bytes 1179656 | tf_op jit(solution)/shard_map/ppermute | solution.py:353
  51.7 4.3 %collective-permute-start.3 = (bf16[1536,128]{1,0:T(8,128)(2,1)S(1)}, bf16[1536,128]{1,0:T(8,128)(2,1)S(1)}, u32[]{:S(2)}, u32[]{:S(2)}) collective-permute-start(bf16[1536,128]{1,0:T(8,128)(2,1)S(1)} %bitcast.29), channel_id=1, source_target_pairs={{0,4},{2,6},{4,0},{6,2},{1,5},{3,7},{5,1},{7,3},{8,12},{10,14},{12... | collective-permute-start | bytes 1179656 | tf_op jit(solution)/shard_map/ppermute | solution.py:353
  56.1 1.9 %collective-permute-start.5 = (bf16[1536,128]{1,0:T(8,128)(2,1)S(1)}, bf16[1536,128]{1,0:T(8,128)(2,1)S(1)}, u32[]{:S(2)}, u32[]{:S(2)}) collective-permute-start(bf16[1536,128]{1,0:T(8,128)(2,1)S(1)} %bitcast.30), channel_id=1, source_target_pairs={{0,6},{2,0},{4,2},{6,4},{1,7},{3,1},{5,3},{7,5},{8,14},{10,8},{12,... | collective-permute-start | bytes 1179656 | tf_op jit(solution)/shard_map/ppermute | solution.py:353
  58.0 1.9 %collective-permute-start = (bf16[1536,128]{1,0:T(8,128)(2,1)S(1)}, bf16[1536,128]{1,0:T(8,128)(2,1)S(1)}, u32[]{:S(2)}, u32[]{:S(2)}) collective-permute-start(bf16[1536,128]{1,0:T(8,128)(2,1)S(1)} %bitcast.31), channel_id=1, source_target_pairs={{0,1},{1,0},{2,3},{3,2},{4,5},{5,4},{6,7},{7,6},{8,9},{9,8},{10,11... | collective-permute-start | bytes 1179656 | tf_op jit(solution)/shard_map/ppermute | solution.py:354
  59.9 3.4 %collective-permute-done.1.rest_2_ = bf16[1536,128]{1,0:T(8,128)(2,1)S(1)} collective-permute-done((bf16[1536,128]{1,0:T(8,128)(2,1)S(1)}, bf16[1536,128]{1,0:T(8,128)(2,1)S(1)}, u32[]{:S(2)}, u32[]{:S(2)}) %collective-permute-start.1) | collective-permute-done | bytes 393248 | tf_op jit(solution)/shard_map/ppermute | solution.py:353
  63.3 1.9 %collective-permute-start.2 = (bf16[1536,128]{1,0:T(8,128)(2,1)S(1)}, bf16[1536,128]{1,0:T(8,128)(2,1)S(1)}, u32[]{:S(2)}, u32[]{:S(2)}) collective-permute-start(bf16[1536,128]{1,0:T(8,128)(2,1)S(1)} %collective-permute-done.1.rest_2_), channel_id=1, source_target_pairs={{0,1},{1,0},{2,3},{3,2},{4,5},{5,4},{6,7},{7,6},{8,9},{9,8},{10,11... | collective-permute-start | bytes 1179656 | tf_op jit(solution)/shard_map/ppermute | solution.py:354
  65.2 2.0 %collective-permute-done.3.rest_4_ = bf16[1536,128]{1,0:T(8,128)(2,1)S(1)} collective-permute-done((bf16[1536,128]{1,0:T(8,128)(2,1)S(1)}, bf16[1536,128]{1,0:T(8,128)(2,1)S(1)}, u32[]{:S(2)}, u32[]{:S(2)}) %collective-permute-start.3) | collective-permute-done | bytes 393248 | tf_op jit(solution)/shard_map/ppermute | solution.py:353
  67.2 1.9 %collective-permute-start.4 = (bf16[1536,128]{1,0:T(8,128)(2,1)S(1)}, bf16[1536,128]{1,0:T(8,128)(2,1)S(1)}, u32[]{:S(2)}, u32[]{:S(2)}) collective-permute-start(bf16[1536,128]{1,0:T(8,128)(2,1)S(1)} %collective-permute-done.3.rest_4_), channel_id=1, source_target_pairs={{0,1},{1,0},{2,3},{3,2},{4,5},{5,4},{6,7},{7,6},{8,9},{9,8},{10,11... | collective-permute-start | bytes 1179656 | tf_op jit(solution)/shard_map/ppermute | solution.py:354
  69.1 3.4 %collective-permute-done.5.rest_6_ = bf16[1536,128]{1,0:T(8,128)(2,1)S(1)} collective-permute-done((bf16[1536,128]{1,0:T(8,128)(2,1)S(1)}, bf16[1536,128]{1,0:T(8,128)(2,1)S(1)}, u32[]{:S(2)}, u32[]{:S(2)}) %collective-permute-start.5) | collective-permute-done | bytes 393248 | tf_op jit(solution)/shard_map/ppermute | solution.py:353
  72.5 1.9 %collective-permute-start.6 = (bf16[1536,128]{1,0:T(8,128)(2,1)S(1)}, bf16[1536,128]{1,0:T(8,128)(2,1)S(1)}, u32[]{:S(2)}, u32[]{:S(2)}) collective-permute-start(bf16[1536,128]{1,0:T(8,128)(2,1)S(1)} %collective-permute-done.5.rest_6_), channel_id=1, source_target_pairs={{0,1},{1,0},{2,3},{3,2},{4,5},{5,4},{6,7},{7,6},{8,9},{9,8},{10,11... | collective-permute-start | bytes 1179656 | tf_op jit(solution)/shard_map/ppermute | solution.py:354
  74.4 0.0 collective-permute-done.rest_1_
  74.5 0.0 collective-permute-done.2.rest_3_
  74.5 0.0 collective-permute-done.4.rest_5_
  74.5 1.7 %collective-permute-done.6.rest_7_ = bf16[1536,128]{1,0:T(8,128)(2,1)S(1)} collective-permute-done((bf16[1536,128]{1,0:T(8,128)(2,1)S(1)}, bf16[1536,128]{1,0:T(8,128)(2,1)S(1)}, u32[]{:S(2)}, u32[]{:S(2)}) %collective-permute-start.6) | collective-permute-done | bytes 393248 | tf_op jit(solution)/shard_map/ppermute | solution.py:354
  76.1 0.0 copy-start
  76.1 0.8 copy-done
  76.9 0.0 all-to-all-done.3.amps
  76.9 0.0 copy-done.2
  76.9 0.0 copy-done.4
  76.9 0.0 copy-start.1
  76.9 1.0 copy-done.1
  77.9 7.0 %multiply.1 = f32[16,24,128]{2,1,0:T(8,128)} custom-call(s32[960]{0:T(1024)S(1)} %copy-done.4, s32[1]{0:T(128)S(6)} %copy.28.slab_a, s32[1]{0:T(128)S(6)} %copy.29.slab_b, s32[1,120]{1,0:T(1,128)S(1)} %bitcast.35, bf16[16,192,128]{2,1,0:T(8,128)(2,1)S(1)} %all-to-all-done.3.amps, bf16[1536,128]{1,0:T(8,128)(2,1)S(1)} %bitcast.32, ...), custom_call_target="tpu_custom_call" | custom-call | tf_op jit(solution)/shard_map/multiply/pallas_call | solution.py:282
  84.9 7.2 %all-to-all-start.5 = ((f32[16,24,128]{2,1,0:T(8,128)}), f32[16,24,128]{2,1,0:T(8,128)S(1)}, u32[]{:S(2)}, u32[]{:S(2)}) async-start(f32[16,24,128]{2,1,0:T(8,128)} %multiply.1), calls=%async_computation.5 | async-start | bytes 393216 | tf_op jit(solution)/shard_map/all_to_all | solution.py:358
  92.8 9.3 %all-to-all-done.5 = f32[16,24,128]{2,1,0:T(8,128)S(1)} async-done(((f32[16,24,128]{2,1,0:T(8,128)}), f32[16,24,128]{2,1,0:T(8,128)S(1)}, u32[]{:S(2)}, u32[]{:S(2)}) %all-to-all-start.5) | async-done | bytes 196640 | tf_op jit(solution)/shard_map/all_to_all | solution.py:358
  102.1 0.0 copy-done.3
  102.1 0.0 copy-done.5
  102.1 2.8 %conditional.1 = (f32[15,8,120]{2,1,0:T(8,128)S(1)}) conditional(s32[]{:T(128)} %bitcast.16, (s32[120]{0:T(128)S(1)}, f32[120]{0:T(128)S(1)}, s32[960]{0:T(1024)S(1)}, s32[1]{0:T(128)}, s32[1]{0:T(128)}, /*index=5*/f32[960]{0:T(1024)S(1)}, f32[16,24,128]{2,1,0:T(8,128)S(1)}, f32[15,8,120]{2,1,0:T(8,128)}) %tuple.28, (s32[1]{0:T(128)}, ...), branch_computations={%region_0.0_spmd, %region_1.3_spmd} | conditional | flops 3319177216 | bytes 84580896 | solution.py:367
  102.1 2.5 %finish.1 = f32[15,8,120]{2,1,0:T(8,128)S(1)} custom-call(s32[960]{0:T(1024)S(1)} %get-tuple-element.42.vir_irrep, s32[120]{0:T(128)S(1)} %get-tuple-element.43.occ_irrep, s32[1]{0:T(128)} %get-tuple-element.44.slab_a, s32[1]{0:T(128)} %get-tuple-element.45.slab_b, f32[120]{0:T(128)S(1)} %get-tuple-element.46.occ_energy, ...), custom_call_target="tpu_custom_call" | custom-call | tf_op jit(solution)/shard_map/cond/branch_0_fun/finish/pallas_call | solution.py:299
  104.8 0.0 copy-start.8
  104.8 0.6 copy-done.8
Async XLA Ops:
  0.0 76.9 %copy-start.2 = (s32[120]{0:T(128)S(1)}, s32[120]{0:T(128)}, u32[]{:S(2)}) copy-start(s32[120]{0:T(128)} %occ_irrep.1) | copy-start | bytes 1444
  0.0 76.9 %copy-start.4 = (s32[960]{0:T(1024)S(1)}, s32[960]{0:T(1024)}, u32[]{:S(2)}) copy-start(s32[960]{0:T(1024)} %vir_irrep.5) | copy-start | bytes 11524
  2.8 36.1 %all-to-all-start.4 = ((bf16[4,384,128]{2,1,0:T(8,128)(2,1)}), bf16[4,384,128]{2,1,0:T(8,128)(2,1)S(1)}, u32[]{:S(2)}, u32[]{:S(2)}) async-start(bf16[4,384,128]{2,1,0:T(8,128)(2,1)} %pack_integrals.1), calls=%async_computation.4 | async-start | bytes 786432 | tf_op jit(solution)/shard_map/all_to_all | solution.py:351
  25.7 76.3 %copy-start.3 = (f32[120]{0:T(128)S(1)}, f32[120]{0:T(128)}, u32[]{:S(2)}) copy-start(f32[120]{0:T(128)} %param.14) | copy-start | bytes 1444
  25.7 76.3 %copy-start.5 = (f32[960]{0:T(1024)S(1)}, f32[960]{0:T(1024)}, u32[]{:S(2)}) copy-start(f32[960]{0:T(1024)} %param.15) | copy-start | bytes 11524
  38.9 38.0 %all-to-all-start.3 = ((bf16[16,192,128]{2,1,0:T(8,128)(2,1)}), bf16[16,192,128]{2,1,0:T(8,128)(2,1)S(1)}, u32[]{:S(2)}, u32[]{:S(2)}) async-start(bf16[16,192,128]{2,1,0:T(8,128)(2,1)} %get-tuple-element.62), calls=%async_computation.3 | async-start | bytes 1572864 | tf_op jit(solution)/shard_map/all_to_all | solution.py:356
  49.3 13.9 %collective-permute-start.1 = (bf16[1536,128]{1,0:T(8,128)(2,1)S(1)}, bf16[1536,128]{1,0:T(8,128)(2,1)S(1)}, u32[]{:S(2)}, u32[]{:S(2)}) collective-permute-start(bf16[1536,128]{1,0:T(8,128)(2,1)S(1)} %bitcast.28), channel_id=1, source_target_pairs={{0,2},{2,4},{4,6},{6,0},{1,3},{3,5},{5,7},{7,1},{8,10},{10,12},{12... | collective-permute-start | bytes 1179656 | tf_op jit(solution)/shard_map/ppermute | solution.py:353
  51.7 15.5 %collective-permute-start.3 = (bf16[1536,128]{1,0:T(8,128)(2,1)S(1)}, bf16[1536,128]{1,0:T(8,128)(2,1)S(1)}, u32[]{:S(2)}, u32[]{:S(2)}) collective-permute-start(bf16[1536,128]{1,0:T(8,128)(2,1)S(1)} %bitcast.29), channel_id=1, source_target_pairs={{0,4},{2,6},{4,0},{6,2},{1,5},{3,7},{5,1},{7,3},{8,12},{10,14},{12... | collective-permute-start | bytes 1179656 | tf_op jit(solution)/shard_map/ppermute | solution.py:353
  56.1 16.5 %collective-permute-start.5 = (bf16[1536,128]{1,0:T(8,128)(2,1)S(1)}, bf16[1536,128]{1,0:T(8,128)(2,1)S(1)}, u32[]{:S(2)}, u32[]{:S(2)}) collective-permute-start(bf16[1536,128]{1,0:T(8,128)(2,1)S(1)} %bitcast.30), channel_id=1, source_target_pairs={{0,6},{2,0},{4,2},{6,4},{1,7},{3,1},{5,3},{7,5},{8,14},{10,8},{12,... | collective-permute-start | bytes 1179656 | tf_op jit(solution)/shard_map/ppermute | solution.py:353
  58.0 16.5 %collective-permute-start = (bf16[1536,128]{1,0:T(8,128)(2,1)S(1)}, bf16[1536,128]{1,0:T(8,128)(2,1)S(1)}, u32[]{:S(2)}, u32[]{:S(2)}) collective-permute-start(bf16[1536,128]{1,0:T(8,128)(2,1)S(1)} %bitcast.31), channel_id=1, source_target_pairs={{0,1},{1,0},{2,3},{3,2},{4,5},{5,4},{6,7},{7,6},{8,9},{9,8},{10,11... | collective-permute-start | bytes 1179656 | tf_op jit(solution)/shard_map/ppermute | solution.py:354
  63.3 11.2 %collective-permute-start.2 = (bf16[1536,128]{1,0:T(8,128)(2,1)S(1)}, bf16[1536,128]{1,0:T(8,128)(2,1)S(1)}, u32[]{:S(2)}, u32[]{:S(2)}) collective-permute-start(bf16[1536,128]{1,0:T(8,128)(2,1)S(1)} %collective-permute-done.1.rest_2_), channel_id=1, source_target_pairs={{0,1},{1,0},{2,3},{3,2},{4,5},{5,4},{6,7},{7,6},{8,9},{9,8},{10,11... | collective-permute-start | bytes 1179656 | tf_op jit(solution)/shard_map/ppermute | solution.py:354
  67.2 7.3 %collective-permute-start.4 = (bf16[1536,128]{1,0:T(8,128)(2,1)S(1)}, bf16[1536,128]{1,0:T(8,128)(2,1)S(1)}, u32[]{:S(2)}, u32[]{:S(2)}) collective-permute-start(bf16[1536,128]{1,0:T(8,128)(2,1)S(1)} %collective-permute-done.3.rest_4_), channel_id=1, source_target_pairs={{0,1},{1,0},{2,3},{3,2},{4,5},{5,4},{6,7},{7,6},{8,9},{9,8},{10,11... | collective-permute-start | bytes 1179656 | tf_op jit(solution)/shard_map/ppermute | solution.py:354
  72.5 3.6 %collective-permute-start.6 = (bf16[1536,128]{1,0:T(8,128)(2,1)S(1)}, bf16[1536,128]{1,0:T(8,128)(2,1)S(1)}, u32[]{:S(2)}, u32[]{:S(2)}) collective-permute-start(bf16[1536,128]{1,0:T(8,128)(2,1)S(1)} %collective-permute-done.5.rest_6_), channel_id=1, source_target_pairs={{0,1},{1,0},{2,3},{3,2},{4,5},{5,4},{6,7},{7,6},{8,9},{9,8},{10,11... | collective-permute-start | bytes 1179656 | tf_op jit(solution)/shard_map/ppermute | solution.py:354
  76.1 0.8 copy-start
  76.9 1.0 copy-start.1
  84.9 17.2 %all-to-all-start.5 = ((f32[16,24,128]{2,1,0:T(8,128)}), f32[16,24,128]{2,1,0:T(8,128)S(1)}, u32[]{:S(2)}, u32[]{:S(2)}) async-start(f32[16,24,128]{2,1,0:T(8,128)} %multiply.1), calls=%async_computation.5 | async-start | bytes 393216 | tf_op jit(solution)/shard_map/all_to_all | solution.py:358
  104.8 0.6 copy-start.8

commit v4 on v3

--- a/solution.py
+++ b/solution.py
@@ -16,8 +16,15 @@
 GROUP = 5
 PARTS = ROWS // GROUP
 STEP = 5
-FAR = 4
-NEAR = 16
+FAR = 8
+NEAR = 8
+ACROSS = 4
+SHARE = SLOTS // ACROSS
+TEAM = NEAR * ACROSS
+BLOCK = 32
+STACK = 4
+TWICE = FAR // STACK
+DEEP = TWICE * PARTS
 REP = 8
 LANES = 128
 BF = jnp.bfloat16
@@ -53,10 +60,11 @@
     return high, middle, low
 
 
-def pack_integrals(place, vir_irrep, slab_b, occ_row, integrals, out, scratch):
+def pack_integrals(place, vir_irrep, slab_b, occ_row, integrals, out, most, scratch):
     red, rep = place()
     occ = occ_row[...]
     occ_col, pos_row, _ = positions(occ)
+    most[0, 0] = jnp.max(pos_row)
     slot = lax.broadcasted_iota(jnp.int32, (SLOTS, O), 0)
     pick = jnp.where(slot == pos_row, 1.0, 0.0).astype(BF)
     b_label = vir_irrep[slab_b[0] * B + rep]
@@ -64,36 +72,40 @@
     for c in range(ROWS):
         label = vir_irrep[red * ROWS + c] ^ b_label
         kept = jnp.where((occ_col ^ label) == occ, integrals[c].astype(F32), 0.0).astype(BF)
-        first = LANES * (c // GROUP) + SLOTS * (c % GROUP)
-        scratch[first : first + SLOTS, :O] = jnp.dot(pick, kept, preferred_element_type=F32)
-    packed = scratch[...].astype(BF)
-    for far in range(FAR):
-        out[far] = packed
+        slots = jnp.dot(pick, kept, preferred_element_type=F32)
+        for x in range(ACROSS):
+            first = (x * PARTS + c // GROUP) * BLOCK + SHARE * (c % GROUP)
+            scratch[first : first + SHARE, :O] = slots[x * SHARE : (x + 1) * SHARE]
+    for x in range(ACROSS):
+        out[x] = scratch[x * PARTS * BLOCK : (x + 1) * PARTS * BLOCK].astype(BF)
 
 
 def pack_amplitudes(
-    place, vir_irrep, occ_irrep, slab_a, occ_row, vir_rows, amplitudes, out, most, starts, chosen, row, packed
+    place, vir_irrep, occ_irrep, slab_a, occ_row, vir_rows, amplitudes, out, starts, chosen, row, packed
 ):
     red, rep = place()
     step = pl.program_id(0)
     occ = occ_row[...]
+    groups = V // GROUP // STACK
+    part = NEAR * PARTS
 
     @pl.when(step == 0)
     def _():
-        _, pos_row, pos_col = positions(occ)
-        most[0, 0] = jnp.max(pos_row)
+        _, _, pos_col = positions(occ)
         lane = lax.broadcasted_iota(jnp.int32, (O, LANES), 1)
         chosen[...] = jnp.zeros_like(chosen)
+        at = pos_col
+        for x in range(1, ACROSS):
+            at += jnp.where(pos_col >= x * SHARE, BLOCK - SHARE, 0)
         for u in range(GROUP):
-            hit = (lane == pos_col + SLOTS * u) & (pos_col < SLOTS)
+            hit = (lane == at + SHARE * u) & (pos_col < SLOTS)
             chosen[u * LANES : u * LANES + O] = jnp.where(hit, 1.0, 0.0).astype(BF)
         labels = vir_rows[...]
         for g in range(9):
             below = jnp.sum(jnp.where(labels < g, 1.0, 0.0), axis=1, keepdims=True)
-            starts[g : g + 1] = jnp.broadcast_to(
-                jnp.sum(below, axis=0, keepdims=True).astype(jnp.int32), (1, LANES)
-            )
-        packed[pl.ds(ROWS, V // GROUP, stride=16), :] = jnp.zeros((V // GROUP, LANES), F32)
+            starts[g : g + 1] = jnp.broadcast_to(below.astype(jnp.int32), (1, LANES))
+        for x in range(ACROSS):
+            packed[x, pl.ds(ROWS, groups, stride=16), :] = jnp.zeros((groups, LANES), F32)
         row[...] = jnp.zeros_like(row)
 
     for j in range(STEP):
@@ -113,67 +125,86 @@
             [row[j, pl.ds(u, V // GROUP, stride=GROUP), :].astype(BF) for u in range(GROUP)], axis=1
         )
         total = jnp.dot(left, chosen[...], preferred_element_type=F32)
-        packed[pl.ds(step * STEP + j, V // GROUP, stride=16), :] = total
+        blocks = [
+            jnp.concatenate([total[(STACK * t + f) * part : (STACK * t + f + 1) * part] for t in range(TWICE)], axis=0)
+            for f in range(STACK)
+        ]
+        place_of = lax.broadcasted_iota(jnp.int32, (groups, LANES), 1) // BLOCK
+        for x in range(ACROSS):
+            tile = blocks[0] if x == 0 else pltpu.roll(blocks[0], (LANES - BLOCK * x), 1)
+            for f in range(1, STACK):
+                moved = blocks[f] if x == f else pltpu.roll(blocks[f], (LANES + BLOCK * (f - x)) % LANES, 1)
+                tile = jnp.where(place_of == f, moved, tile)
+            packed[x, pl.ds(step * STEP + j, groups, stride=16), :] = tile
 
     @pl.when(step == ROWS // STEP - 1)
     def _():
         rows = PARTS * 16
         for e in range(NEAR):
-            for far in range(FAR):
-                first = (far * NEAR + e) * rows
-                out[e, far * rows : (far + 1) * rows] = packed[first : first + rows].astype(BF)
+            for x in range(ACROSS):
+                for t in range(TWICE):
+                    first = (t * NEAR + e) * rows
+                    out[ACROSS * e + x, t * rows : (t + 1) * rows] = packed[x, first : first + rows].astype(BF)
 
 
 def slot_owner(place, slot):
     _, rep = place()
-    return ((rep // 2 + (REP // 2 - slot // 2)) % (REP // 2)) * 2 + (rep + slot) % 2
+    return slot % ACROSS * 2 + (rep + slot // ACROSS) % 2
 
 
 def multiply(place, vir_irrep, slab_a, slab_b, occ_row, amps, *rest):
-    ints, (out, left, held, sems) = rest[:REP], rest[REP:]
+    ints, (out, kept, picks) = rest[:2], rest[2:]
     red, rep = place()
-    copies = [pltpu.make_async_copy(ints[slot], held.at[slot], sems.at[slot]) for slot in range(REP)]
-    for copy in copies:
-        copy.start()
     occ = occ_row[...]
-    rows = NEAR * 16
-    for s in range(NEAR):
-        for block in range(FAR * PARTS):
-            left[s * 16 : (s + 1) * 16, block * LANES : (block + 1) * LANES] = amps[
-                s, block * 16 : (block + 1) * 16
-            ]
+    rows = TEAM * 16
+    left = jnp.concatenate([amps[:, k * 16 : (k + 1) * 16].reshape(rows, LANES) for k in range(DEEP)], axis=1)
     _, _, pos_col = positions(occ)
     occ_lanes = jnp.concatenate([occ, jnp.full((1, LANES - O), 64, jnp.int32)], axis=1)
     pos_lanes = jnp.concatenate([pos_col, jnp.full((LANES - O, 1), -4 * LANES, jnp.int32)], axis=0)
     row = lax.broadcasted_iota(jnp.int32, (rows, LANES), 0)
-    local = (row // 16) * ROWS + row % 16
-    second = local >= O
-    i_index = jnp.where(second, local - O, local)
-    i_label = jnp.zeros((rows, LANES), jnp.int32)
+    i_index = (row // (16 * ACROSS)) * ROWS + row % 16
+    row_label = jnp.zeros((rows, LANES), jnp.int32)
     for g in range(1, 8):
         start = jnp.sum(jnp.where(occ < g, 1.0, 0.0), axis=1, keepdims=True).astype(jnp.int32)
-        i_label += jnp.where(i_index >= start, 1, 0)
-    a_first = slab_a[0] * A + (rep * FAR + red // NEAR) * 2
-    row_label = i_label ^ jnp.where(second, vir_irrep[a_first + 1], vir_irrep[a_first])
+        row_label += jnp.where(i_index >= start, 1, 0)
+    a_label = jnp.zeros((rows, LANES), jnp.int32)
+    for x in range(ACROSS):
+        label = vir_irrep[slab_a[0] * A + (x * 2 + rep % 2) * FAR + red // NEAR]
+        a_label = jnp.where((row // 16) % ACROSS == x, label, a_label)
+    row_label = row_label ^ a_label
     wanted = row_label ^ occ_lanes
     lane = lax.broadcasted_iota(jnp.int32, (LANES, 2 * LANES), 1)
-    total = jnp.zeros((rows, 2 * LANES), F32)
+    for slot in range(REP):
+        pick = jnp.where(lane == pos_lanes + SLOTS * slot, 1.0, 0.0).astype(BF)
+        for piece in range(2):
+            first = (2 * slot + piece) * LANES
+            picks[first : first + LANES] = pick
     for pair in range(REP // 2):
-        copies[2 * pair].wait()
-        copies[2 * pair + 1].wait()
-        right = jnp.concatenate([held[2 * pair], held[2 * pair + 1]], axis=1)
-        both = jnp.dot(left[...], right, preferred_element_type=F32)
+        held = ints[pair * 2 // ACROSS]
+        across = (pair * 2 % ACROSS, pair * 2 % ACROSS + 1)
+        right = jnp.concatenate(
+            [
+                jnp.concatenate([held[far, x, g * BLOCK : (g + 1) * BLOCK] for x in across], axis=1)
+                for t in range(TWICE)
+                for g in range(PARTS)
+                for far in range(t * STACK, (t + 1) * STACK)
+            ],
+            axis=0,
+        )
+        both = jnp.dot(left, right, preferred_element_type=F32)
         for half in range(2):
             slot = 2 * pair + half
             b_label = vir_irrep[slab_b[0] * B + slot_owner(place, slot)]
             part = both[:, half * LANES : (half + 1) * LANES]
             part = jnp.where(wanted == b_label, part, 0.0)
-            pick = jnp.where(lane == pos_lanes + SLOTS * slot, 1.0, 0.0).astype(BF)
-            for piece in thirds(part):
-                total += jnp.dot(piece, pick, preferred_element_type=F32)
+            high = part.astype(BF)
+            first = 2 * slot * LANES
+            kept[:, first : first + LANES] = high
+            kept[:, first + LANES : first + 2 * LANES] = (part - high.astype(F32)).astype(BF)
+    total = jnp.dot(kept[...], picks[...], preferred_element_type=F32)
     rest = total[:, LANES:]
     moved = pltpu.roll(rest, LANES // 2, 1)
-    for e in range(NEAR):
+    for e in range(TEAM):
         out[e, :16] = total[e * 16 : (e + 1) * 16, :LANES]
         out[e, 16:] = rest[e * 16 : e * 16 + 8] + moved[e * 16 + 8 : e * 16 + 16]
 
@@ -185,7 +216,7 @@
     occ = occ_row[...]
     _, pos_row, _ = positions(occ)
     total = parts[0]
-    for s in range(1, NEAR):
+    for s in range(1, TEAM):
         total += parts[s]
     main = total[:16]
     rest = jnp.concatenate([total[16:], pltpu.roll(total[16:], LANES // 2, 1)], axis=0)
@@ -239,10 +270,10 @@
 def call_pack_integrals(place, vir_irrep, slab_b, occ_row, integrals, **kw):
     return pl.pallas_call(
         functools.partial(pack_integrals, place),
-        out_shape=jax.ShapeDtypeStruct((FAR, PARTS * LANES, LANES), BF),
+        out_shape=(jax.ShapeDtypeStruct((ACROSS, PARTS * BLOCK, LANES), BF), jax.ShapeDtypeStruct((1, 1), jnp.int32)),
         in_specs=[SMEM, SMEM, VMEM, VMEM],
-        out_specs=VMEM,
-        scratch_shapes=[pltpu.VMEM((PARTS * LANES, LANES), F32)],
+        out_specs=(VMEM, SMEM),
+        scratch_shapes=[pltpu.VMEM((ACROSS * PARTS * BLOCK, LANES), F32)],
         compiler_params=params(16),
         cost_estimate=pl.CostEstimate(flops=2 * 10**7, bytes_accessed=600000, transcendentals=0),
         name="pack_integrals",
@@ -257,20 +288,17 @@
 def call_pack_amplitudes(place, vir_irrep, occ_irrep, slab_a, occ_row, vir_rows, amplitudes, **kw):
     return pl.pallas_call(
         functools.partial(pack_amplitudes, place),
-        out_shape=(
-            jax.ShapeDtypeStruct((NEAR, FAR * PARTS * 16, LANES), BF),
-            jax.ShapeDtypeStruct((1, 1), jnp.int32),
-        ),
+        out_shape=jax.ShapeDtypeStruct((TEAM, DEEP * 16, LANES), BF),
         grid=(ROWS // STEP,),
-        in_specs=[SMEM, SMEM, SMEM, fixed((1, O)), fixed((B, O)), pl.BlockSpec((STEP, V, O), lambda r: (r, 0, 0))],
-        out_specs=(fixed((NEAR, FAR * PARTS * 16, LANES)), SMEM),
+        in_specs=[SMEM, SMEM, SMEM, fixed((1, O)), fixed((1, V)), pl.BlockSpec((STEP, V, O), lambda r: (r, 0, 0))],
+        out_specs=fixed((TEAM, DEEP * 16, LANES)),
         scratch_shapes=[
             pltpu.VMEM((16, LANES), jnp.int32),
             pltpu.VMEM((GROUP * LANES, LANES), BF),
             pltpu.VMEM((STEP, V, LANES), F32),
-            pltpu.VMEM((V // GROUP * 16, LANES), F32),
+            pltpu.VMEM((ACROSS, V // GROUP // STACK * 16, LANES), F32),
         ],
-        compiler_params=params(32),
+        compiler_params=params(16),
         cost_estimate=pl.CostEstimate(flops=10**9, bytes_accessed=4500000, transcendentals=0),
         name="pack_amplitudes",
         **kw,
@@ -278,18 +306,16 @@
 
 
 def call_multiply(place, vir_irrep, slab_a, slab_b, occ_row, amps, ints, **kw):
-    depth = FAR * PARTS * LANES
     return pl.pallas_call(
         functools.partial(multiply, place),
-        out_shape=jax.ShapeDtypeStruct((NEAR, 24, LANES), F32),
-        in_specs=[SMEM, SMEM, SMEM, VMEM, VMEM] + [pl.BlockSpec(memory_space=pl.ANY)] * REP,
+        out_shape=jax.ShapeDtypeStruct((TEAM, 24, LANES), F32),
+        in_specs=[SMEM, SMEM, SMEM, VMEM, VMEM] + [VMEM] * 2,
         out_specs=VMEM,
         scratch_shapes=[
-            pltpu.VMEM((NEAR * 16, depth), BF),
-            pltpu.VMEM((REP, depth, LANES), BF),
-            pltpu.SemaphoreType.DMA((REP,)),
+            pltpu.VMEM((TEAM * 16, 2 * REP * LANES), BF),
+            pltpu.VMEM((2 * REP * LANES, 2 * LANES), BF),
         ],
-        compiler_params=params(32),
+        compiler_params=params(24),
         name="multiply",
         **kw,
     )(vir_irrep, slab_a, slab_b, occ_row, amps, *ints)
@@ -342,36 +368,37 @@
     return jnp.where(allowed, updated, jnp.zeros_like(updated))
 
 
+def packed_form(
+    amplitudes, integrals, other_terms, occ_energy, vir_energy, occ_irrep, vir_irrep, slab_a, slab_b, ints
+):
+    occ_row = occ_irrep.reshape(1, O)
+    vir_rows = vir_irrep.reshape(1, V)
+    ints = lax.all_to_all(ints, "x", 0, 0, tiled=True)
+    amps = call_pack_amplitudes(own_place, vir_irrep, occ_irrep, slab_a, occ_row, vir_rows, amplitudes)
+    ints = lax.all_gather(ints, "far", axis=0)
+    ints, amps = lax.optimization_barrier((ints, amps))
+    ints = [ints, lax.ppermute(ints, "core", [(0, 1), (1, 0)])]
+    amps = lax.all_to_all(amps, ("near", "x"), 0, 0, tiled=True)
+    parts = call_multiply(own_place, vir_irrep, slab_a, slab_b, occ_row, amps, ints)
+    parts = lax.all_to_all(parts, ("near", "x"), 0, 0, tiled=True)
+    return call_finish(
+        own_place, vir_irrep, occ_irrep, slab_a, slab_b, occ_energy, vir_energy,
+        occ_row, occ_energy.reshape(1, O), parts, other_terms,
+    )
+
+
 def on_device(
     amplitudes, integrals, other_terms, occ_energy, vir_energy, occ_irrep, vir_irrep, slab_a, slab_b
 ):
-    occ_row = occ_irrep.reshape(1, O)
-    vir_rows = vir_irrep.reshape(B, O)
-    ints = call_pack_integrals(own_place, vir_irrep, slab_b, occ_row, integrals.reshape(ROWS, O, O))
-    ints = lax.all_to_all(ints, "far", 0, 0, tiled=True).reshape(FAR * PARTS * LANES, LANES)
-    count = REP // 2
-    held = [ints] + [lax.ppermute(ints, "x", [(i, (i + s) % count) for i in range(count)]) for s in range(1, count)]
-    ints = [half for own in held for half in (own, lax.ppermute(own, "core", [(0, 1), (1, 0)]))]
-    amps, most = call_pack_amplitudes(own_place, vir_irrep, occ_irrep, slab_a, occ_row, vir_rows, amplitudes)
-    amps = lax.all_to_all(amps, "near", 0, 0, tiled=True)
-    parts = call_multiply(own_place, vir_irrep, slab_a, slab_b, occ_row, amps, ints)
-    parts = lax.all_to_all(parts, "near", 0, 0, tiled=True)
-
-    def packed_form(amplitudes, integrals, *rest):
-        other_terms, occ_energy, vir_energy, occ_irrep, vir_irrep, slab_a, slab_b, parts = rest
-        return call_finish(
-            own_place, vir_irrep, occ_irrep, slab_a, slab_b, occ_energy, vir_energy,
-            occ_irrep.reshape(1, O), occ_energy.reshape(1, O), parts, other_terms,
-        )
-
-    return lax.cond(
-        most[0, 0] >= SLOTS, lambda *args: whole_form(*args[:-1]), packed_form,
-        amplitudes, integrals, other_terms, occ_energy, vir_energy, occ_irrep, vir_irrep, slab_a, slab_b, parts,
+    args = (amplitudes, integrals, other_terms, occ_energy, vir_energy, occ_irrep, vir_irrep, slab_a, slab_b)
+    ints, most = call_pack_integrals(
+        own_place, vir_irrep, slab_b, occ_irrep.reshape(1, O), integrals.reshape(ROWS, O, O)
     )
+    return lax.cond(most[0, 0] >= SLOTS, lambda *rest: whole_form(*rest[:-1]), packed_form, *args, ints)
 
 
 def solution(mesh):
-    split = Mesh(mesh.devices.reshape(FAR, NEAR, REP // 2, 2), ("far", "near", "x", "core"))
+    split = Mesh(mesh.devices.reshape(FAR, NEAR, ACROSS, 2), ("far", "near", "x", "core"))
     rows = P(("x", "core", "far", "near"), None, None)
     placed = (
         rows,

time: 107 us -> 94.1 us (0.88)
  blocking collectives: 0 us -> 47.9 us
  starting transfers between devices: 49 us -> 19.5 us
  waiting for transfers between devices: 32.9 us -> 7.71 us
  local copies, waits for them, and re-layouts: 3.15 us -> 0.64 us
  Pallas kernels: 18 us -> 15.7 us
    all_gather x0 -> x1, blocking collectives: none -> 34.3 us  [packed_form(): ints = lax.all_gather(ints, 'far', axis=0)]
    all_to_all x3 -> x2, waiting for transfers between devices: 22.5 us -> 5.46 us  [the longest x1 5.45 us: packed_form(): amps = lax.all_to_all(amps, ('near', 'x'), 0, 0, tiled=True)]
    all_to_all x3 -> x2, starting transfers between devices: 32.7 us -> 17.6 us  [the longest x1 9.14 us: packed_form(): ints = lax.all_to_all(ints, 'x', 0, 0, tiled=True)]
    ppermute x7 -> x1, starting transfers between devices: 16.3 us -> 1.92 us  [packed_form(): ints = [ints, lax.ppermute(ints, 'core', [(0, 1), (1, 0)])]]
    all_to_all x0 -> x1, blocking collectives: none -> 13.6 us  [packed_form(): parts = lax.all_to_all(parts, ('near', 'x'), 0, 0, tiled=True)]
    ppermute x7 -> x1, waiting for transfers between devices: 10.4 us -> 2.25 us  [packed_form(): ints = [ints, lax.ppermute(ints, 'core', [(0, 1), (1, 0)])]]
    pallas_call x1, Pallas kernels: 6.98 us -> 4 us  [call_multiply(): pl.pallas_call(functools.partial(multiply, place), out_shape=jax.ShapeDty...]
    unnamed x14 -> x2, local copies, waits for them, and re-layouts: 2.39 us -> 0.62 us
  transfers between devices with their start and end apart: 10 -> 3, of which waited for: 6 -> 2; matrix products, arithmetic and copies ran while one was open for 1% -> 0% of each run, Pallas kernels for 6% -> 8%
where the time goes in v4:
time: 94.1 us; the launch traced here: 93.2 us
  blocking collectives  47.9 us (51%)
  starting transfers between devices  19.5 us (21%)
  Pallas kernels  15.7 us (17%)
  waiting for transfers between devices  7.71 us (8%)
  between operations  1.33 us (1%)
    all_gather x1, blocking collectives, packed_form(): ints = lax.all_gather(ints, 'far', axis=0)  34.3 us
    all_to_all x1, blocking collectives, packed_form(): parts = lax.all_to_all(parts, ('near', 'x'), 0, 0, tiled=True)  13.6 us
    all_to_all x1, starting transfers between devices, packed_form(): ints = lax.all_to_all(ints, 'x', 0, 0, tiled=True)  9.14 us
    all_to_all x1, starting transfers between devices, packed_form(): amps = lax.all_to_all(amps, ('near', 'x'), 0, 0, tiled=True)  8.45 us
    pallas_call x1, Pallas kernels, call_pack_amplitudes(): pl.pallas_call(functools.partial(pack_amplitudes, place), out_shape=jax.S...  7.34 us
    all_to_all x1, waiting for transfers between devices, packed_form(): amps = lax.all_to_all(amps, ('near', 'x'), 0, 0, tiled=True)  5.45 us
    pallas_call x1, Pallas kernels, call_multiply(): pl.pallas_call(functools.partial(multiply, place), out_shape=jax.ShapeDty...  4 us
    pallas_call x1, Pallas kernels, call_finish(): pl.pallas_call(functools.partial(finish, place), out_shape=jax.ShapeDtype...  2.37 us
  transfers between devices with their start and end apart: 3, of which 2 were waited for; matrix products, arithmetic and copies ran while one was open for 0% of the time, Pallas kernels for 8%

profile of v4, /device:TPU:6, one launch (start us, length us, event | category | flops | bytes accessed | tf_op | source)
XLA Modules:
  0.0 93.2 jit_solution(9426069766356599630)
XLA Ops:
  0.7 2.0 %pack_integrals.1 = (bf16[4,96,128]{2,1,0:T(8,128)(2,1)}, s32[1,1]{1,0:T(1,128)}) custom-call(s32[960]{0:T(1024)} %vir_irrep.1, s32[1]{0:T(128)S(6)} %copy.28.slab_b, s32[1,120]{1,0:T(1,128)} %bitcast.31, bf16[15,120,120]{2,1,0:T(8,128)(2,1)} %bitcast.37), custom_call_target="tpu_custom_call" | custom-call | flops 20000000 | bytes 600000 | tf_op jit(solution)/shard_map/pack_integrals/pallas_call | solution.py:271
  3.4 89.2 %conditional.1 = (f32[15,8,120]{2,1,0:T(8,128)S(1)}) conditional(s32[]{:T(128)} %bitcast.19, (s32[120]{0:T(128)}, f32[120]{0:T(128)}, bf16[4,96,128]{2,1,0:T(8,128)(2,1)}, s32[960]{0:T(1024)}, s32[1]{0:T(128)}, /*index=5*/bf16[15,960,120]{2,1,0:T(8,128)(2,1)}, s32[1]{0:T(128)}, f32[960]{0:T(1024)}, f32[15,8,120]{2,1,0:T(8,128)}) %tuple.12, ...), branch_computations={%region_0.0_spmd, %region_1.3_spmd} | conditional | flops 3319177216 | bytes 84615568 | solution.py:397
  3.4 0.0 copy-start
  3.4 0.0 copy-start.4
  3.4 9.1 %all-to-all-start = ((bf16[4,96,128]{2,1,0:T(8,128)(2,1)}), bf16[4,96,128]{2,1,0:T(8,128)(2,1)S(1)}, u32[]{:S(2)}, u32[]{:S(2)}) async-start(bf16[4,96,128]{2,1,0:T(8,128)(2,1)} %get-tuple-element.50), calls=%async_computation | async-start | bytes 196608 | tf_op jit(solution)/shard_map/cond/branch_0_fun/all_to_all | solution.py:376
  12.5 7.3 %pack_amplitudes.1 = bf16[32,96,128]{2,1,0:T(8,128)(2,1)} custom-call(s32[960]{0:T(1024)} %get-tuple-element.44.vir_irrep, s32[120]{0:T(128)} %get-tuple-element.45.occ_irrep, s32[1]{0:T(128)} %get-tuple-element.46.slab_a, s32[1,120]{1,0:T(1,128)} %bitcast.32, s32[1,960]{1,0:T(1,128)} %bitcast.36, bf16[15,960,120]{2,1,0:T(8,128)(2,1)} %get-tuple-element.51.amplitudes), custom_call_target="tpu_custom_call" | custom-call | flops 1000000000 | bytes 4500000 | tf_op jit(solution)/shard_map/cond/branch_0_fun/pack_amplitudes/pallas_call | solution.py:289
  19.9 0.0 copy-start.2
  19.9 0.0 copy-start.6
  19.9 0.0 copy-start.9
  19.9 0.0 all-to-all-done
  19.9 34.3 %all-gather = bf16[32,96,128]{2,1,0:T(8,128)(2,1)S(1)} all-gather(bf16[4,96,128]{2,1,0:T(8,128)(2,1)S(1)} %all-to-all-done), channel_id=2, replica_groups=mesh['far'=8,'near'=8,'x'=4,'core'=2] {'far'}, dimensions={0}, use_global_device_ids=true | all-gather | bytes 884736 | tf_op jit(solution)/shard_map/cond/branch_0_fun/all_gather | solution.py:378
  54.2 8.5 %all-to-all-start.1 = ((bf16[32,96,128]{2,1,0:T(8,128)(2,1)}), bf16[32,96,128]{2,1,0:T(8,128)(2,1)S(1)}, u32[]{:S(2)}, u32[]{:S(2)}) async-start(bf16[32,96,128]{2,1,0:T(8,128)(2,1)} %pack_amplitudes.1), calls=%async_computation.1 | async-start | bytes 1572864 | tf_op jit(solution)/shard_map/cond/branch_0_fun/all_to_all | solution.py:381
  62.7 1.9 %collective-permute-start = (bf16[8,4,96,128]{3,2,1,0:T(8,128)(2,1)S(1)}, bf16[8,4,96,128]{3,2,1,0:T(8,128)(2,1)S(1)}, u32[]{:S(2)}, u32[]{:S(2)}) collective-permute-start(bf16[8,4,96,128]{3,2,1,0:T(8,128)(2,1)S(1)} %bitcast.29), channel_id=1, source_target_pairs={{0,1},{1,0},{2,3},{3,2},{4,5},{5,4},{6,7},{7,6},{8,9},{9,8},{10,11... | collective-permute-start | bytes 2359304 | tf_op jit(solution)/shard_map/cond/branch_0_fun/ppermute | solution.py:380
  64.6 2.3 %collective-permute-done.rest_1_ = bf16[8,4,96,128]{3,2,1,0:T(8,128)(2,1)S(1)} collective-permute-done((bf16[8,4,96,128]{3,2,1,0:T(8,128)(2,1)S(1)}, bf16[8,4,96,128]{3,2,1,0:T(8,128)(2,1)S(1)}, u32[]{:S(2)}, u32[]{:S(2)}) %collective-permute-start) | collective-permute-done | bytes 786464 | tf_op jit(solution)/shard_map/cond/branch_0_fun/ppermute | solution.py:380
  66.9 5.5 %all-to-all-done.1.amps = bf16[32,96,128]{2,1,0:T(8,128)(2,1)S(1)} async-done(((bf16[32,96,128]{2,1,0:T(8,128)(2,1)}), bf16[32,96,128]{2,1,0:T(8,128)(2,1)S(1)}, u32[]{:S(2)}, u32[]{:S(2)}) %all-to-all-start.1) | async-done | bytes 786464 | tf_op jit(solution)/shard_map/cond/branch_0_fun/all_to_all | solution.py:381
  72.3 0.0 copy-done
  72.3 0.0 copy-done.4
  72.3 4.0 %multiply.1 = f32[32,24,128]{2,1,0:T(8,128)S(1)} custom-call(s32[960]{0:T(1024)S(1)} %copy-done.4, s32[1]{0:T(128)} %get-tuple-element.46.slab_a, s32[1]{0:T(128)} %get-tuple-element.47.slab_b, s32[1,120]{1,0:T(1,128)S(1)} %bitcast.33, bf16[32,96,128]{2,1,0:T(8,128)(2,1)S(1)} %all-to-all-done.1.amps, bf16[8,4,96,128]{3,2,1,0:T(8,128)(2,1)S(1)} %bitcast.30, ...), custom_call_target="tpu_custom_call" | custom-call | tf_op jit(solution)/shard_map/cond/branch_0_fun/multiply/pallas_call | solution.py:309
  76.3 13.6 %all_to_all.32.parts = f32[32,24,128]{2,1,0:T(8,128)S(1)} all-to-all(f32[32,24,128]{2,1,0:T(8,128)S(1)} %multiply.1), channel_id=1, replica_groups=mesh['far'=8,'near'=8,'x'=4,'core'=2] {'near','x'}, dimensions={0} | all-to-all | bytes 786432 | tf_op jit(solution)/shard_map/cond/branch_0_fun/all_to_all | solution.py:383
  89.9 0.0 copy-done.2
  89.9 0.0 copy-done.6
  89.9 0.0 copy-done.9
  89.9 2.4 %finish.1 = f32[15,8,120]{2,1,0:T(8,128)S(1)} custom-call(s32[960]{0:T(1024)S(1)} %copy-done.4, s32[120]{0:T(128)S(1)} %copy-done, s32[1]{0:T(128)} %get-tuple-element.46.slab_a, s32[1]{0:T(128)} %get-tuple-element.47.slab_b, f32[120]{0:T(128)S(1)} %copy-done.2, f32[960]{0:T(1024)S(1)} %copy-done.6, s32[1,120]{1,0:T(1,128)S(1)} %bitcast.34, ...), custom_call_target="tpu_custom_call" | custom-call | tf_op jit(solution)/shard_map/cond/branch_0_fun/finish/pallas_call | solution.py:325
  92.5 0.0 copy-start.11
  92.5 0.6 copy-done.11
Async XLA Ops:
  3.4 69.0 %copy-start = (s32[120]{0:T(128)S(1)}, s32[120]{0:T(128)}, u32[]{:S(2)}) copy-start(s32[120]{0:T(128)} %get-tuple-element.45.occ_irrep) | copy-start | bytes 1444 | tf_op jit(solution)/shard_map/cond
  3.4 69.0 %copy-start.4 = (s32[960]{0:T(1024)S(1)}, s32[960]{0:T(1024)}, u32[]{:S(2)}) copy-start(s32[960]{0:T(1024)} %get-tuple-element.44.vir_irrep) | copy-start | bytes 11524 | tf_op jit(solution)/shard_map/cond
  3.4 16.5 %all-to-all-start = ((bf16[4,96,128]{2,1,0:T(8,128)(2,1)}), bf16[4,96,128]{2,1,0:T(8,128)(2,1)S(1)}, u32[]{:S(2)}, u32[]{:S(2)}) async-start(bf16[4,96,128]{2,1,0:T(8,128)(2,1)} %get-tuple-element.50), calls=%async_computation | async-start | bytes 196608 | tf_op jit(solution)/shard_map/cond/branch_0_fun/all_to_all | solution.py:376
  19.9 70.1 %copy-start.2 = (f32[120]{0:T(128)S(1)}, f32[120]{0:T(128)}, u32[]{:S(2)}) copy-start(f32[120]{0:T(128)} %get-tuple-element.48.occ_energy) | copy-start | bytes 1444 | tf_op jit(solution)/shard_map/cond
  19.9 70.1 %copy-start.6 = (f32[960]{0:T(1024)S(1)}, f32[960]{0:T(1024)}, u32[]{:S(2)}) copy-start(f32[960]{0:T(1024)} %get-tuple-element.49.vir_energy) | copy-start | bytes 11524 | tf_op jit(solution)/shard_map/cond
  19.9 70.1 %copy-start.9 = (f32[15,8,120]{2,1,0:T(8,128)S(1)}, f32[15,8,120]{2,1,0:T(8,128)}, u32[]{:S(2)}) copy-start(f32[15,8,120]{2,1,0:T(8,128)} %get-tuple-element.54.other) | copy-start | bytes 172804 | tf_op jit(solution)/shard_map/cond
  54.2 18.1 %all-to-all-start.1 = ((bf16[32,96,128]{2,1,0:T(8,128)(2,1)}), bf16[32,96,128]{2,1,0:T(8,128)(2,1)S(1)}, u32[]{:S(2)}, u32[]{:S(2)}) async-start(bf16[32,96,128]{2,1,0:T(8,128)(2,1)} %pack_amplitudes.1), calls=%async_computation.1 | async-start | bytes 1572864 | tf_op jit(solution)/shard_map/cond/branch_0_fun/all_to_all | solution.py:381
  62.7 4.2 %collective-permute-start = (bf16[8,4,96,128]{3,2,1,0:T(8,128)(2,1)S(1)}, bf16[8,4,96,128]{3,2,1,0:T(8,128)(2,1)S(1)}, u32[]{:S(2)}, u32[]{:S(2)}) collective-permute-start(bf16[8,4,96,128]{3,2,1,0:T(8,128)(2,1)S(1)} %bitcast.29), channel_id=1, source_target_pairs={{0,1},{1,0},{2,3},{3,2},{4,5},{5,4},{6,7},{7,6},{8,9},{9,8},{10,11... | collective-permute-start | bytes 2359304 | tf_op jit(solution)/shard_map/cond/branch_0_fun/ppermute | solution.py:380
  92.5 0.6 copy-start.11

commit v5 on v4

--- a/solution.py
+++ b/solution.py
@@ -60,13 +60,13 @@
     return high, middle, low
 
 
-def pack_integrals(place, vir_irrep, slab_b, occ_row, integrals, out, most, scratch):
+def pack_integrals(place, window, vir_irrep, slab_b, occ_row, integrals, out, most, scratch):
     red, rep = place()
     occ = occ_row[...]
     occ_col, pos_row, _ = positions(occ)
     most[0, 0] = jnp.max(pos_row)
     slot = lax.broadcasted_iota(jnp.int32, (SLOTS, O), 0)
-    pick = jnp.where(slot == pos_row, 1.0, 0.0).astype(BF)
+    pick = jnp.where(slot == pos_row - SLOTS * window, 1.0, 0.0).astype(BF)
     b_label = vir_irrep[slab_b[0] * B + rep]
     scratch[...] = jnp.zeros_like(scratch)
     for c in range(ROWS):
@@ -81,7 +81,7 @@
 
 
 def pack_amplitudes(
-    place, vir_irrep, occ_irrep, slab_a, occ_row, vir_rows, amplitudes, out, starts, chosen, row, packed
+    place, window, vir_irrep, occ_irrep, slab_a, occ_row, vir_rows, amplitudes, out, starts, chosen, row, packed
 ):
     red, rep = place()
     step = pl.program_id(0)
@@ -92,13 +92,14 @@
     @pl.when(step == 0)
     def _():
         _, _, pos_col = positions(occ)
+        pos_col -= SLOTS * window
         lane = lax.broadcasted_iota(jnp.int32, (O, LANES), 1)
         chosen[...] = jnp.zeros_like(chosen)
         at = pos_col
         for x in range(1, ACROSS):
             at += jnp.where(pos_col >= x * SHARE, BLOCK - SHARE, 0)
         for u in range(GROUP):
-            hit = (lane == at + SHARE * u) & (pos_col < SLOTS)
+            hit = (lane == at + SHARE * u) & (pos_col >= 0) & (pos_col < SLOTS)
             chosen[u * LANES : u * LANES + O] = jnp.where(hit, 1.0, 0.0).astype(BF)
         labels = vir_rows[...]
         for g in range(9):
@@ -108,6 +109,7 @@
             packed[x, pl.ds(ROWS, groups, stride=16), :] = jnp.zeros((groups, LANES), F32)
         row[...] = jnp.zeros_like(row)
 
+    c_index = lax.broadcasted_iota(jnp.int16, (V, O), 0)
     for j in range(STEP):
         row_id = (rep * (FAR * NEAR) + red) * ROWS + step * STEP + j
         label = vir_irrep[slab_a[0] * A + row_id // O] ^ occ_irrep[row_id % O]
@@ -117,9 +119,8 @@
         for g in range(8):
             low = jnp.where(partner == g, starts[g : g + 1, :O], low)
             high = jnp.where(partner == g, starts[g + 1 : g + 2, :O], high)
-        c_index = lax.broadcasted_iota(jnp.int32, (V, O), 0)
-        kept = (c_index >= low) & (c_index < high)
-        row[j, :, :O] = jnp.where(kept, amplitudes[j].astype(F32), 0.0)
+        kept = (c_index >= low.astype(jnp.int16)) & (c_index < high.astype(jnp.int16))
+        row[j, :, :O] = jnp.where(kept, amplitudes[j], jnp.zeros((), BF)).astype(F32)
     for j in range(STEP):
         left = jnp.concatenate(
             [row[j, pl.ds(u, V // GROUP, stride=GROUP), :].astype(BF) for u in range(GROUP)], axis=1
@@ -129,7 +130,7 @@
             jnp.concatenate([total[(STACK * t + f) * part : (STACK * t + f + 1) * part] for t in range(TWICE)], axis=0)
             for f in range(STACK)
         ]
-        place_of = lax.broadcasted_iota(jnp.int32, (groups, LANES), 1) // BLOCK
+        place_of = lax.broadcasted_iota(jnp.int32, (1, LANES), 1) // BLOCK
         for x in range(ACROSS):
             tile = blocks[0] if x == 0 else pltpu.roll(blocks[0], (LANES - BLOCK * x), 1)
             for f in range(1, STACK):
@@ -152,7 +153,7 @@
     return slot % ACROSS * 2 + (rep + slot // ACROSS) % 2
 
 
-def multiply(place, vir_irrep, slab_a, slab_b, occ_row, amps, *rest):
+def multiply(place, window, vir_irrep, slab_a, slab_b, occ_row, amps, *rest):
     ints, (out, kept, picks) = rest[:2], rest[2:]
     red, rep = place()
     occ = occ_row[...]
@@ -160,6 +161,8 @@
     left = jnp.concatenate([amps[:, k * 16 : (k + 1) * 16].reshape(rows, LANES) for k in range(DEEP)], axis=1)
     _, _, pos_col = positions(occ)
     occ_lanes = jnp.concatenate([occ, jnp.full((1, LANES - O), 64, jnp.int32)], axis=1)
+    pos_col -= SLOTS * window
+    pos_col = jnp.where((pos_col >= 0) & (pos_col < SLOTS), pos_col, -4 * LANES)
     pos_lanes = jnp.concatenate([pos_col, jnp.full((LANES - O, 1), -4 * LANES, jnp.int32)], axis=0)
     row = lax.broadcasted_iota(jnp.int32, (rows, LANES), 0)
     i_index = (row // (16 * ACROSS)) * ROWS + row % 16
@@ -210,28 +213,33 @@
 
 
 def finish(
-    place, vir_irrep, occ_irrep, slab_a, slab_b, occ_energy, vir_energy, occ_row, energy_row, parts, other, out, cycle
+    place, vir_irrep, occ_irrep, slab_a, slab_b, occ_energy, vir_energy, occ_row, energy_row, other, *rest
 ):
+    windows, (out, cycle) = rest[:-2], rest[-2:]
     red, rep = place()
     occ = occ_row[...]
     _, pos_row, _ = positions(occ)
-    total = parts[0]
-    for s in range(1, TEAM):
-        total += parts[s]
-    main = total[:16]
-    rest = jnp.concatenate([total[16:], pltpu.roll(total[16:], LANES // 2, 1)], axis=0)
-    mains = jnp.concatenate(thirds(main), axis=0)
-    rests = jnp.concatenate(thirds(rest), axis=0)
     lane = lax.broadcasted_iota(jnp.int32, (LANES, O), 0)
+    values = [jnp.zeros((48, O), F32) for _ in range(REP)]
+    for window, parts in enumerate(windows):
+        total = parts[0]
+        for s in range(1, TEAM):
+            total += parts[s]
+        main = total[:16]
+        rest = jnp.concatenate([total[16:], pltpu.roll(total[16:], LANES // 2, 1)], axis=0)
+        mains = jnp.concatenate(thirds(main), axis=0)
+        rests = jnp.concatenate(thirds(rest), axis=0)
+        at = pos_row - SLOTS * window
+        at = jnp.where((at >= 0) & (at < SLOTS), at, -4 * LANES)
+        for slot in range(REP):
+            if SLOTS * slot < LANES:
+                pick = jnp.where(lane == at + SLOTS * slot, 1.0, 0.0).astype(BF)
+                values[slot] += jnp.dot(mains, pick, preferred_element_type=F32)
+            if SLOTS * (slot + 1) > LANES:
+                pick = jnp.where((lane == at + (SLOTS * slot - LANES)) & (lane < LANES // 2), 1.0, 0.0).astype(BF)
+                values[slot] += jnp.dot(rests, pick, preferred_element_type=F32)
     for slot in range(REP):
-        value = jnp.zeros((48, O), F32)
-        if SLOTS * slot < LANES:
-            pick = jnp.where(lane == pos_row + SLOTS * slot, 1.0, 0.0).astype(BF)
-            value += jnp.dot(mains, pick, preferred_element_type=F32)
-        if SLOTS * (slot + 1) > LANES:
-            at = pos_row + (SLOTS * slot - LANES)
-            pick = jnp.where((lane == at) & (lane < LANES // 2), 1.0, 0.0).astype(BF)
-            value += jnp.dot(rests, pick, preferred_element_type=F32)
+        value = values[slot]
         cycle[pl.ds(slot_owner(place, slot), 16, stride=B), :O] = (value[:16] + value[16:32]) + value[32:]
     b_first = slab_b[0] * B
     b_index = lax.broadcasted_iota(jnp.int32, (B, 1), 0)
@@ -267,9 +275,9 @@
     return pltpu.CompilerParams(vmem_limit_bytes=limit * 1024 * 1024)
 
 
-def call_pack_integrals(place, vir_irrep, slab_b, occ_row, integrals, **kw):
+def call_pack_integrals(place, window, vir_irrep, slab_b, occ_row, integrals):
     return pl.pallas_call(
-        functools.partial(pack_integrals, place),
+        functools.partial(pack_integrals, place, window),
         out_shape=(jax.ShapeDtypeStruct((ACROSS, PARTS * BLOCK, LANES), BF), jax.ShapeDtypeStruct((1, 1), jnp.int32)),
         in_specs=[SMEM, SMEM, VMEM, VMEM],
         out_specs=(VMEM, SMEM),
@@ -277,7 +285,6 @@
         compiler_params=params(16),
         cost_estimate=pl.CostEstimate(flops=2 * 10**7, bytes_accessed=600000, transcendentals=0),
         name="pack_integrals",
-        **kw,
     )(vir_irrep, slab_b, occ_row, integrals)
 
 
@@ -285,9 +292,9 @@
     return pl.BlockSpec(shape, lambda step: (0,) * len(shape))
 
 
-def call_pack_amplitudes(place, vir_irrep, occ_irrep, slab_a, occ_row, vir_rows, amplitudes, **kw):
+def call_pack_amplitudes(place, window, vir_irrep, occ_irrep, slab_a, occ_row, vir_rows, amplitudes):
     return pl.pallas_call(
-        functools.partial(pack_amplitudes, place),
+        functools.partial(pack_amplitudes, place, window),
         out_shape=jax.ShapeDtypeStruct((TEAM, DEEP * 16, LANES), BF),
         grid=(ROWS // STEP,),
         in_specs=[SMEM, SMEM, SMEM, fixed((1, O)), fixed((1, V)), pl.BlockSpec((STEP, V, O), lambda r: (r, 0, 0))],
@@ -301,13 +308,12 @@
         compiler_params=params(16),
         cost_estimate=pl.CostEstimate(flops=10**9, bytes_accessed=4500000, transcendentals=0),
         name="pack_amplitudes",
-        **kw,
     )(vir_irrep, occ_irrep, slab_a, occ_row, vir_rows, amplitudes)
 
 
-def call_multiply(place, vir_irrep, slab_a, slab_b, occ_row, amps, ints, **kw):
+def call_multiply(place, window, vir_irrep, slab_a, slab_b, occ_row, amps, ints):
     return pl.pallas_call(
-        functools.partial(multiply, place),
+        functools.partial(multiply, place, window),
         out_shape=jax.ShapeDtypeStruct((TEAM, 24, LANES), F32),
         in_specs=[SMEM, SMEM, SMEM, VMEM, VMEM] + [VMEM] * 2,
         out_specs=VMEM,
@@ -317,21 +323,21 @@
         ],
         compiler_params=params(24),
         name="multiply",
-        **kw,
     )(vir_irrep, slab_a, slab_b, occ_row, amps, *ints)
 
 
-def call_finish(place, vir_irrep, occ_irrep, slab_a, slab_b, occ_energy, vir_energy, occ_row, energy_row, parts, other, **kw):
+def call_finish(
+    place, vir_irrep, occ_irrep, slab_a, slab_b, occ_energy, vir_energy, occ_row, energy_row, other, windows
+):
     return pl.pallas_call(
         functools.partial(finish, place),
         out_shape=jax.ShapeDtypeStruct((ROWS, B, O), F32),
-        in_specs=[SMEM] * 6 + [VMEM] * 4,
+        in_specs=[SMEM] * 6 + [VMEM] * (3 + len(windows)),
         out_specs=VMEM,
         scratch_shapes=[pltpu.VMEM((16 * B, LANES), F32)],
         compiler_params=params(16),
         name="finish",
-        **kw,
-    )(vir_irrep, occ_irrep, slab_a, slab_b, occ_energy, vir_energy, occ_row, energy_row, parts, other)
+    )(vir_irrep, occ_irrep, slab_a, slab_b, occ_energy, vir_energy, occ_row, energy_row, other, *windows)
 
 
 def whole_form(amplitudes, integrals, other_terms, occ_energy, vir_energy, occ_irrep, vir_irrep, slab_a, slab_b):
@@ -369,21 +375,29 @@
 
 
 def packed_form(
-    amplitudes, integrals, other_terms, occ_energy, vir_energy, occ_irrep, vir_irrep, slab_a, slab_b, ints
+    count, amplitudes, integrals, other_terms, occ_energy, vir_energy, occ_irrep, vir_irrep, slab_a, slab_b, ints
 ):
     occ_row = occ_irrep.reshape(1, O)
     vir_rows = vir_irrep.reshape(1, V)
-    ints = lax.all_to_all(ints, "x", 0, 0, tiled=True)
-    amps = call_pack_amplitudes(own_place, vir_irrep, occ_irrep, slab_a, occ_row, vir_rows, amplitudes)
-    ints = lax.all_gather(ints, "far", axis=0)
-    ints, amps = lax.optimization_barrier((ints, amps))
-    ints = [ints, lax.ppermute(ints, "core", [(0, 1), (1, 0)])]
-    amps = lax.all_to_all(amps, ("near", "x"), 0, 0, tiled=True)
-    parts = call_multiply(own_place, vir_irrep, slab_a, slab_b, occ_row, amps, ints)
-    parts = lax.all_to_all(parts, ("near", "x"), 0, 0, tiled=True)
+    windows = [None] * count
+    for window in range(count):
+        if window > 0:
+            ints, _ = call_pack_integrals(
+                own_place, window, vir_irrep, slab_b, occ_row, integrals.reshape(ROWS, O, O)
+            )
+        ints = lax.all_to_all(ints, "x", 0, 0, tiled=True)
+        amps = call_pack_amplitudes(own_place, window, vir_irrep, occ_irrep, slab_a, occ_row, vir_rows, amplitudes)
+        ints = lax.all_gather(ints, "far", axis=0)
+        ints, amps = lax.optimization_barrier((ints, amps))
+        both = [ints, lax.ppermute(ints, "core", [(0, 1), (1, 0)])]
+        amps = lax.all_to_all(amps, ("near", "x"), 0, 0, tiled=True)
+        for col in range(count):
+            part = call_multiply(own_place, col, vir_irrep, slab_a, slab_b, occ_row, amps, both)
+            windows[col] = part if windows[col] is None else windows[col] + part
+    windows = [lax.all_to_all(part, ("near", "x"), 0, 0, tiled=True) for part in windows]
     return call_finish(
         own_place, vir_irrep, occ_irrep, slab_a, slab_b, occ_energy, vir_energy,
-        occ_row, occ_energy.reshape(1, O), parts, other_terms,
+        occ_row, occ_energy.reshape(1, O), other_terms, windows,
     )
 
 
@@ -392,9 +406,18 @@
 ):
     args = (amplitudes, integrals, other_terms, occ_energy, vir_energy, occ_irrep, vir_irrep, slab_a, slab_b)
     ints, most = call_pack_integrals(
-        own_place, vir_irrep, slab_b, occ_irrep.reshape(1, O), integrals.reshape(ROWS, O, O)
+        own_place, 0, vir_irrep, slab_b, occ_irrep.reshape(1, O), integrals.reshape(ROWS, O, O)
     )
-    return lax.cond(most[0, 0] >= SLOTS, lambda *rest: whole_form(*rest[:-1]), packed_form, *args, ints)
+
+    def crowded(*rest):
+        return lax.cond(
+            most[0, 0] >= 2 * SLOTS,
+            lambda *last: whole_form(*last[:-1]),
+            functools.partial(packed_form, 2),
+            *rest,
+        )
+
+    return lax.cond(most[0, 0] >= SLOTS, crowded, functools.partial(packed_form, 1), *args, ints)
 
 
 def solution(mesh):

time: 94.1 us -> 93.4 us (level)
  transfers between devices with their start and end apart: 3 -> 3, of which waited for: 2 -> 2; matrix products, arithmetic and copies ran while one was open for 0% -> 0% of each run, Pallas kernels for 8% -> 7%
where the time goes in v5:
time: 93.4 us; the launch traced here: 92.4 us
  blocking collectives  48 us (51%)
  starting transfers between devices  19.6 us (21%)
  Pallas kernels  15.7 us (17%)
  waiting for transfers between devices  7.71 us (8%)
  between operations  1.33 us (1%)
    all_gather x1, blocking collectives, packed_form(): ints = lax.all_gather(ints, 'far', axis=0)  34.4 us
    all_to_all x1, blocking collectives, packed_form(): lax.all_to_all(part, ('near', 'x'), 0, 0, tiled=True)  13.6 us
    all_to_all x1, starting transfers between devices, packed_form(): ints = lax.all_to_all(ints, 'x', 0, 0, tiled=True)  9.14 us
    all_to_all x1, starting transfers between devices, packed_form(): amps = lax.all_to_all(amps, ('near', 'x'), 0, 0, tiled=True)  8.51 us
    pallas_call x1, Pallas kernels, call_pack_amplitudes(): pl.pallas_call(functools.partial(pack_amplitudes, place, window), out_sha...  6.63 us
    all_to_all x1, waiting for transfers between devices, packed_form(): amps = lax.all_to_all(amps, ('near', 'x'), 0, 0, tiled=True)  5.45 us
    pallas_call x1, Pallas kernels, call_multiply(): pl.pallas_call(functools.partial(multiply, place, window), out_shape=jax....  3.99 us
    pallas_call x1, Pallas kernels, call_finish(): pl.pallas_call(functools.partial(finish, place), out_shape=jax.ShapeDtype...  3 us
  transfers between devices with their start and end apart: 3, of which 2 were waited for; matrix products, arithmetic and copies ran while one was open for 0% of the time, Pallas kernels for 7%

profile of v5, /device:TPU:6, one launch (start us, length us, event | category | flops | bytes accessed | tf_op | source)
XLA Modules:
  0.0 92.4 jit_solution(1406813210518179454)
XLA Ops:
  0.7 2.1 %pack_integrals.3 = (bf16[4,96,128]{2,1,0:T(8,128)(2,1)}, s32[1,1]{1,0:T(1,128)}) custom-call(s32[960]{0:T(1024)} %vir_irrep.1, s32[1]{0:T(128)S(6)} %copy.29.slab_b, s32[1,120]{1,0:T(1,128)} %bitcast.43, bf16[15,120,120]{2,1,0:T(8,128)(2,1)} %bitcast.60), custom_call_target="tpu_custom_call" | custom-call | flops 20000000 | bytes 600000 | tf_op jit(solution)/shard_map/pack_integrals/pallas_call | solution.py:279
  3.4 89.0 %conditional.2 = (f32[15,8,120]{2,1,0:T(8,128)}) conditional(s32[]{:T(128)} %bitcast.26, (s32[120]{0:T(128)}, f32[120]{0:T(128)}, bf16[4,96,128]{2,1,0:T(8,128)(2,1)}, s32[960]{0:T(1024)}, s32[1]{0:T(128)}, /*index=5*/bf16[15,960,120]{2,1,0:T(8,128)(2,1)}, s32[1]{0:T(128)}, f32[960]{0:T(1024)}, f32[15,8,120]{2,1,0:T(8,128)}) %tuple.20, ...), branch_computations={%region_0.0_spmd, %region_1.5_spmd} | conditional | flops 3319177216 | bytes 89634864 | solution.py:420
  3.4 0.0 copy-start.8
  3.4 0.0 copy-start.12
  3.4 9.1 %all-to-all-start = ((bf16[4,96,128]{2,1,0:T(8,128)(2,1)}), bf16[4,96,128]{2,1,0:T(8,128)(2,1)S(1)}, u32[]{:S(2)}, u32[]{:S(2)}) async-start(bf16[4,96,128]{2,1,0:T(8,128)(2,1)} %get-tuple-element.96), calls=%async_computation | async-start | bytes 196608 | tf_op jit(solution)/shard_map/cond/branch_0_fun/all_to_all | solution.py:388
  12.6 6.6 %pack_amplitudes.3 = bf16[32,96,128]{2,1,0:T(8,128)(2,1)} custom-call(s32[960]{0:T(1024)} %get-tuple-element.88.vir_irrep, s32[120]{0:T(128)} %get-tuple-element.90.occ_irrep, s32[1]{0:T(128)} %get-tuple-element.91.slab_a, s32[1,120]{1,0:T(1,128)} %bitcast.44, s32[1,960]{1,0:T(1,128)} %bitcast.57, bf16[15,960,120]{2,1,0:T(8,128)(2,1)} %get-tuple-element.97.amplitudes), custom_call_target="tpu_custom_call" | custom-call | flops 1000000000 | bytes 4500000 | tf_op jit(solution)/shard_map/cond/branch_0_fun/pack_amplitudes/pallas_call | solution.py:296
  19.2 0.0 copy-start.10
  19.2 0.0 copy-start.14
  19.2 0.0 copy-start.17
  19.2 0.0 all-to-all-done
  19.2 34.4 %all-gather = bf16[32,96,128]{2,1,0:T(8,128)(2,1)S(1)} all-gather(bf16[4,96,128]{2,1,0:T(8,128)(2,1)S(1)} %all-to-all-done), channel_id=2, replica_groups=mesh['far'=8,'near'=8,'x'=4,'core'=2] {'far'}, dimensions={0}, use_global_device_ids=true | all-gather | bytes 884736 | tf_op jit(solution)/shard_map/cond/branch_0_fun/all_gather | solution.py:390
  53.6 8.5 %all-to-all-start.1 = ((bf16[32,96,128]{2,1,0:T(8,128)(2,1)}), bf16[32,96,128]{2,1,0:T(8,128)(2,1)S(1)}, u32[]{:S(2)}, u32[]{:S(2)}) async-start(bf16[32,96,128]{2,1,0:T(8,128)(2,1)} %pack_amplitudes.3), calls=%async_computation.1 | async-start | bytes 1572864 | tf_op jit(solution)/shard_map/cond/branch_0_fun/all_to_all | solution.py:393
  62.2 1.9 %collective-permute-start = (bf16[8,4,96,128]{3,2,1,0:T(8,128)(2,1)S(1)}, bf16[8,4,96,128]{3,2,1,0:T(8,128)(2,1)S(1)}, u32[]{:S(2)}, u32[]{:S(2)}) collective-permute-start(bf16[8,4,96,128]{3,2,1,0:T(8,128)(2,1)S(1)} %bitcast.41), channel_id=1, source_target_pairs={{0,1},{1,0},{2,3},{3,2},{4,5},{5,4},{6,7},{7,6},{8,9},{9,8},{10,11... | collective-permute-start | bytes 2359304 | tf_op jit(solution)/shard_map/cond/branch_0_fun/ppermute | solution.py:392
  64.1 2.3 %collective-permute-done.rest_1_ = bf16[8,4,96,128]{3,2,1,0:T(8,128)(2,1)S(1)} collective-permute-done((bf16[8,4,96,128]{3,2,1,0:T(8,128)(2,1)S(1)}, bf16[8,4,96,128]{3,2,1,0:T(8,128)(2,1)S(1)}, u32[]{:S(2)}, u32[]{:S(2)}) %collective-permute-start) | collective-permute-done | bytes 786464 | tf_op jit(solution)/shard_map/cond/branch_0_fun/ppermute | solution.py:392
  66.3 5.5 %all-to-all-done.1.amps = bf16[32,96,128]{2,1,0:T(8,128)(2,1)S(1)} async-done(((bf16[32,96,128]{2,1,0:T(8,128)(2,1)}), bf16[32,96,128]{2,1,0:T(8,128)(2,1)S(1)}, u32[]{:S(2)}, u32[]{:S(2)}) %all-to-all-start.1) | async-done | bytes 786464 | tf_op jit(solution)/shard_map/cond/branch_0_fun/all_to_all | solution.py:393
  71.8 0.0 copy-done.8
  71.8 0.0 copy-done.12
  71.8 4.0 %multiply.5 = f32[32,24,128]{2,1,0:T(8,128)S(1)} custom-call(s32[960]{0:T(1024)S(1)} %copy-done.12, s32[1]{0:T(128)} %get-tuple-element.91.slab_a, s32[1]{0:T(128)} %get-tuple-element.92.slab_b, s32[1,120]{1,0:T(1,128)S(1)} %bitcast.45, bf16[32,96,128]{2,1,0:T(8,128)(2,1)S(1)} %all-to-all-done.1.amps, bf16[8,4,96,128]{3,2,1,0:T(8,128)(2,1)S(1)} %bitcast.42, ...), custom_call_target="tpu_custom_call" | custom-call | tf_op jit(solution)/shard_map/cond/branch_0_fun/multiply/pallas_call | solution.py:315
  75.8 13.6 %all_to_all.56.rest_0_ = f32[32,24,128]{2,1,0:T(8,128)S(1)} all-to-all(f32[32,24,128]{2,1,0:T(8,128)S(1)} %multiply.5), channel_id=1, replica_groups=mesh['far'=8,'near'=8,'x'=4,'core'=2] {'near','x'}, dimensions={0} | all-to-all | bytes 786432 | tf_op jit(solution)/shard_map/cond/branch_0_fun/all_to_all | solution.py:397
  89.4 0.0 copy-done.10
  89.4 0.0 copy-done.14
  89.4 0.0 copy-done.17
  89.4 3.0 %finish.2 = f32[15,8,120]{2,1,0:T(8,128)} custom-call(s32[960]{0:T(1024)S(1)} %copy-done.12, s32[120]{0:T(128)S(1)} %copy-done.8, s32[1]{0:T(128)} %get-tuple-element.91.slab_a, s32[1]{0:T(128)} %get-tuple-element.92.slab_b, f32[120]{0:T(128)S(1)} %copy-done.10, f32[960]{0:T(1024)S(1)} %copy-done.14, s32[1,120]{1,0:T(1,128)S(1)} %bitcast.46, ...), custom_call_target="tpu_custom_call" | custom-call | tf_op jit(solution)/shard_map/cond/branch_0_fun/finish/pallas_call | solution.py:332
Async XLA Ops:
  3.4 68.4 %copy-start.8 = (s32[120]{0:T(128)S(1)}, s32[120]{0:T(128)}, u32[]{:S(2)}) copy-start(s32[120]{0:T(128)} %get-tuple-element.90.occ_irrep) | copy-start | bytes 1444 | tf_op jit(solution)/shard_map/cond
  3.4 68.4 %copy-start.12 = (s32[960]{0:T(1024)S(1)}, s32[960]{0:T(1024)}, u32[]{:S(2)}) copy-start(s32[960]{0:T(1024)} %get-tuple-element.88.vir_irrep) | copy-start | bytes 11524 | tf_op jit(solution)/shard_map/cond
  3.4 15.8 %all-to-all-start = ((bf16[4,96,128]{2,1,0:T(8,128)(2,1)}), bf16[4,96,128]{2,1,0:T(8,128)(2,1)S(1)}, u32[]{:S(2)}, u32[]{:S(2)}) async-start(bf16[4,96,128]{2,1,0:T(8,128)(2,1)} %get-tuple-element.96), calls=%async_computation | async-start | bytes 196608 | tf_op jit(solution)/shard_map/cond/branch_0_fun/all_to_all | solution.py:388
  19.2 70.2 %copy-start.10 = (f32[120]{0:T(128)S(1)}, f32[120]{0:T(128)}, u32[]{:S(2)}) copy-start(f32[120]{0:T(128)} %get-tuple-element.93.occ_energy) | copy-start | bytes 1444 | tf_op jit(solution)/shard_map/cond
  19.2 70.2 %copy-start.14 = (f32[960]{0:T(1024)S(1)}, f32[960]{0:T(1024)}, u32[]{:S(2)}) copy-start(f32[960]{0:T(1024)} %get-tuple-element.94.vir_energy) | copy-start | bytes 11524 | tf_op jit(solution)/shard_map/cond
  19.2 70.2 %copy-start.17 = (f32[15,8,120]{2,1,0:T(8,128)S(1)}, f32[15,8,120]{2,1,0:T(8,128)}, u32[]{:S(2)}) copy-start(f32[15,8,120]{2,1,0:T(8,128)} %get-tuple-element.95.other) | copy-start | bytes 172804 | tf_op jit(solution)/shard_map/cond
  53.6 18.2 %all-to-all-start.1 = ((bf16[32,96,128]{2,1,0:T(8,128)(2,1)}), bf16[32,96,128]{2,1,0:T(8,128)(2,1)S(1)}, u32[]{:S(2)}, u32[]{:S(2)}) async-start(bf16[32,96,128]{2,1,0:T(8,128)(2,1)} %pack_amplitudes.3), calls=%async_computation.1 | async-start | bytes 1572864 | tf_op jit(solution)/shard_map/cond/branch_0_fun/all_to_all | solution.py:393
  62.2 4.2 %collective-permute-start = (bf16[8,4,96,128]{3,2,1,0:T(8,128)(2,1)S(1)}, bf16[8,4,96,128]{3,2,1,0:T(8,128)(2,1)S(1)}, u32[]{:S(2)}, u32[]{:S(2)}) collective-permute-start(bf16[8,4,96,128]{3,2,1,0:T(8,128)(2,1)S(1)} %bitcast.41), channel_id=1, source_target_pairs={{0,1},{1,0},{2,3},{3,2},{4,5},{5,4},{6,7},{7,6},{8,9},{9,8},{10,11... | collective-permute-start | bytes 2359304 | tf_op jit(solution)/shard_map/cond/branch_0_fun/ppermute | solution.py:392
